TPU v7x, 128 devices: a whole 4x4x4 slice. The times are simulated.
128 devices in a mesh: seq: 64 (over y, z, x), head: 2 (over core).
Axes of the slice: x: 4, y: 4, z: 4, core: 2. Of those that a mesh axis runs over, the one named last changes fastest.
Arguments:
- image_qkv: bfloat16 [3, 7680, 2432], P(None, 'seq', 'head'), may hold values from -10 to 10
- text_qkv: bfloat16 [3, 512, 2432], P(None, 'seq', 'head'), may hold values from -5 to 5
- image_grad: bfloat16 [7680, 2432], P('seq', 'head'), may hold values from -6 to 6
- text_grad: bfloat16 [512, 2432], P('seq', 'head'), may hold values from -6 to 6
- text_len: int32 [1], replicated, may hold values from 64 to 512
Outputs:
- image_dqkv: bfloat16 [3, 7680, 2432], P(None, 'seq', 'head')
- text_dqkv: bfloat16 [3, 512, 2432], P(None, 'seq', 'head')
All inputs are finite; a program needn't handle non-finite values.
Results may differ from a plain program's by a relative error of at most 0.0095.
Values may be sent and summed in bfloat16 or wider, within the bound.
A program may use at most 128 MiB of HBM per device.

v0:
```python
import jax
import jax.numpy as jnp
from jax import lax
from jax.sharding import PartitionSpec as P

HEAD_DIM = 64


def partner_2(x, axis, stride):
    return lax.ppermute(x, axis, [(i, i ^ 1 << stride) for i in range(lax.axis_size(axis))])


def split_heads(block, head_dim):
    shape = block.shape
    heads = shape[-1] // head_dim
    moved = block.reshape(shape[:-1] + (heads, head_dim))
    return jnp.moveaxis(moved, -2, -3)


def join_heads(block):
    heads, count, width = block.shape
    return jnp.moveaxis(block, 0, 1).reshape(count, heads * width)


def gather_bits(block, bits, mover):
    position = lax.axis_index("seq")
    for bit in bits:
        partner = mover(block, bit)
        upper = position >> bit & 1 == 1
        block = jnp.where(
            upper, jnp.concatenate([partner, block], 1), jnp.concatenate([block, partner], 1)
        )
    return block


def halve_bits(block, bits, mover, axis):
    position = lax.axis_index("seq")
    for bit in reversed(bits):
        half = block.shape[axis] // 2
        lower = lax.slice_in_dim(block, 0, half, axis=axis)
        higher = lax.slice_in_dim(block, half, 2 * half, axis=axis)
        upper = position >> bit & 1 == 1
        keep = jnp.where(upper, higher, lower)
        send = jnp.where(upper, lower, higher)
        block = keep + mover(send, bit)
    return block


def merge_bits(stats, bits, mover, combine):
    for bit in bits:
        stats = combine(stats, mover(stats, bit))
    return stats


def merge_softmax(first, second):
    top = jnp.maximum(first[0], second[0])
    left = jnp.exp(first[0] - top)
    right = jnp.exp(second[0] - top)
    rest = first[1:] * left[None] + second[1:] * right[None]
    return jnp.concatenate([top[None], rest], 0)


def add_stats(first, second):
    return first + second


def body(image_qkv, text_qkv, image_grad, text_grad, text_len):
    count = lax.axis_size("seq")
    bits = count.bit_length() - 1
    row_bits = bits // 2
    position = lax.axis_index("seq")
    row_group = 1 << row_bits
    col_group = count >> row_bits
    low_bits = list(range(row_bits))
    high_bits = list(range(row_bits, bits))
    image_rows = image_qkv.shape[1]
    text_rows = text_qkv.shape[1]
    scale = HEAD_DIM ** (-0.5)
    queries = jnp.concatenate([image_qkv[0], text_qkv[0]], 0)
    keys = jnp.concatenate([image_qkv[1], text_qkv[1]], 0)
    values = jnp.concatenate([image_qkv[2], text_qkv[2]], 0)
    grads = jnp.concatenate([image_grad, text_grad], 0)
    query_side = gather_bits(
        jnp.stack([queries, grads]), low_bits, lambda x, bit: partner_2(x, "seq", bit)
    )
    key_side = gather_bits(
        jnp.stack([keys, values]), high_bits, lambda x, bit: partner_2(x, "seq", bit)
    )
    column = jnp.arange(col_group, dtype=jnp.int32)
    owner = column * row_group + (position & row_group - 1)
    text_index = owner[:, None] * text_rows + jnp.arange(text_rows, dtype=jnp.int32)[None, :]
    text_valid = text_index < text_len[0]
    mask = jnp.concatenate([jnp.ones((col_group, image_rows), bool), text_valid], 1).reshape(-1)
    query_heads = split_heads(query_side, HEAD_DIM)
    key_heads = split_heads(key_side, HEAD_DIM)

    def scores_of(query, key_h):
        scores = jnp.einsum("qd,kd->qk", query, key_h, preferred_element_type=jnp.float32) * scale
        return jnp.where(mask[None, :], scores, -jnp.inf)

    def dprobs_of(grad, value):
        return jnp.einsum("qd,kd->qk", grad, value, preferred_element_type=jnp.float32)

    operands = (query_heads[0], query_heads[1], key_heads[0], key_heads[1])

    def max_sum(items):
        query, grad, key_h, value = items
        scores = scores_of(query, key_h)
        top = jnp.max(scores, 1)
        return jnp.stack([top, jnp.sum(jnp.exp(scores - top[:, None]), 1)])

    partial_value = jnp.moveaxis(lax.map(max_sum, operands), 1, 0)
    merged = merge_bits(
        partial_value, low_bits, lambda x, bit: partner_2(x, "seq", bit), merge_softmax
    )
    lse = merged[0] + jnp.log(merged[1])

    def weighted_sum(items):
        query, grad, key_h, value, lse_h = items
        probs = jnp.exp(scores_of(query, key_h) - lse_h[:, None])
        return jnp.sum(probs * dprobs_of(grad, value), 1)

    weights = lax.map(weighted_sum, operands + (lse,))
    delta = merge_bits(weights, low_bits, lambda x, bit: partner_2(x, "seq", bit), add_stats)

    def gradients(items):
        query, grad, key_h, value, lse_h, delta_h = items
        probs = jnp.exp(scores_of(query, key_h) - lse_h[:, None])
        dprobs = dprobs_of(grad, value)
        grad_v = jnp.einsum(
            "qk,qd->kd", probs.astype(jnp.bfloat16), grad, preferred_element_type=jnp.float32
        )
        dscore = (probs * (dprobs - delta_h[:, None]) * scale).astype(jnp.bfloat16)
        grad_q = jnp.einsum("qk,kd->qd", dscore, key_h, preferred_element_type=jnp.float32)
        grad_k = jnp.einsum("qk,qd->kd", dscore, query, preferred_element_type=jnp.float32)
        return (grad_q, grad_k, grad_v)

    grad_q, grad_k, grad_v = lax.map(gradients, operands + (lse, delta))
    query_part = join_heads(grad_q)
    key_part = jnp.stack([join_heads(grad_k), join_heads(grad_v)])
    own_query = halve_bits(query_part, low_bits, lambda x, bit: partner_2(x, "seq", bit), 0)
    own_keys = halve_bits(
        key_part,
        high_bits,
        lambda x, bit: partner_2(x.astype(jnp.bfloat16), "seq", bit).astype(x.dtype),
        1,
    )
    image_out = jnp.stack(
        [own_query[:image_rows], own_keys[0, :image_rows], own_keys[1, :image_rows]]
    )
    text_out = jnp.stack(
        [own_query[image_rows:], own_keys[0, image_rows:], own_keys[1, image_rows:]]
    )
    return (image_out.astype(jnp.bfloat16), text_out.astype(jnp.bfloat16))


def solution(mesh):
    return jax.shard_map(
        body,
        mesh=mesh,
        in_specs=(
            P(None, "seq", "head"),
            P(None, "seq", "head"),
            P("seq", "head"),
            P("seq", "head"),
            P(),
        ),
        out_specs=(P(None, "seq", "head"), P(None, "seq", "head")),
        check_vma=False,
    )
```

profile of v0, /device:TPU:0, one launch (start us, length us, event | category | flops | bytes accessed | tf_op | source)
XLA Modules:
  0.0 628.5 jit_solution(7034506863759758995)
XLA Ops:
  4.8 4.0 collective-permute-start.3
  13.1 10.0 %collective-permute-done.3 = bf16[2,128,1216]{1,2,0:T(8,128)(2,1)} collective-permute-done((bf16[2,128,1216]{1,2,0:T(8,128)(2,1)}, bf16[2,128,1216]{1,2,0:T(8,128)(2,1)}, u32[]{:S(2)}, u32[]{:S(2)}) %collective-permute-start.3) | collective-permute-done | bytes 622624 | tf_op jit(solution)/shard_map/ppermute | solution.py:10
  27.5 2.9 maximum_select_fusion.6
  30.3 3.0 collective-permute-start.1
  33.4 21.3 %collective-permute-done.4 = bf16[2,256,1216]{1,2,0:T(8,128)(2,1)S(1)} collective-permute-done((bf16[2,256,1216]{1,2,0:T(8,128)(2,1)}, bf16[2,256,1216]{1,2,0:T(8,128)(2,1)S(1)}, u32[]{:S(2)}, u32[]{:S(2)}) %collective-permute-start.4) | collective-permute-done | bytes 1245216 | tf_op jit(solution)/shard_map/ppermute | solution.py:10
  54.7 3.4 maximum_select_fusion.4
  58.1 3.2 collective-permute-start.5
  61.3 3.4 maximum_select_fusion.2
  74.5 39.8 %collective-permute-done.5 = bf16[2,512,1216]{1,2,0:T(8,128)(2,1)} collective-permute-done((bf16[2,512,1216]{1,2,0:T(8,128)(2,1)}, bf16[2,512,1216]{1,2,0:T(8,128)(2,1)}, u32[]{:S(2)}, u32[]{:S(2)}) %collective-permute-start.5) | collective-permute-done | bytes 2490400 | tf_op jit(solution)/shard_map/ppermute | solution.py:10
  114.2 4.4 fusion.54
  120.6 4.3 fusion.53
  124.9 2.8 slice_bitcast_fusion.1
  127.7 5.7 copy.60
  133.5 5.7 copy.61
  139.2 54.3 %while.34 = (s32[]{:T(128)}, f32[19,2,1024]{2,0,1:T(8,128)S(1)}, pred[8,128]{1,0:T(8,128)(4,1)S(1)}, bf16[19,1024,64]{2,1,0:T(8,128)(2,1)}, bf16[19,1024,64]{2,1,0:T(8,128)(2,1)}, /*index=5*/s32[]{:T(128)}, s32[]{:T(128)}) while((s32[]{:T(128)}, f32[19,2,1024]{2,0,1:T(8,128)S(1)}, pred[8,128]{1,0:T(8,128)(4,1)S(1)}, ...), condition=%wide.region_3.4_spmd, body=%wide.region_0.3_spmd.sunk | while | flops 141557760 | bytes 8977497 | solution.py:112
  195.1 4.2 collective-permute-done.6
  199.4 3.6 collective-permute-start.7
  202.9 3.7 collective-permute-done.7
  207.6 4.0 copy.63
  211.7 5.7 copy.62
  217.4 78.3 %while.35 = (s32[]{:T(128)}, f32[19,1024]{1,0:T(8,128)S(1)}, pred[8,128]{1,0:T(8,128)(4,1)S(1)}, bf16[19,1024,64]{2,1,0:T(8,128)(2,1)}, bf16[19,1024,64]{2,1,0:T...) while((s32[]{:T(128)}, f32[19,1024]{1,0:T(8,128)S(1)}, ...), condition=%wide.region_6.7_spmd, body=%wide.region_4.6_spmd.sunk | while | flops 273677312 | bytes 9464949 | solution.py:123
  300.4 4.2 collective-permute-start.10
  308.7 3.5 collective-permute-done.11
  312.2 217.4 %while.36 = (s32[]{:T(128)}, f32[19,1024,64]{1,2,0:T(8,128)}, f32[19,1024,64]{1,2,0:T(8,128)}, f32[19,1024,64]{1,2,0:T(8,128)}, pred[8,128]{1,0:T(8,128)(4,1)S(1...) while((s32[]{:T(128)}, f32[19,1024,64]{1,2,0:T(8,128)}, ...), condition=%wide.region_8.9_spmd, body=%wide.region_7.8_spmd.sunk | while | flops 682622976 | bytes 21531776 | solution.py:138
  529.6 3.3 slice_select_fusion.1
  535.9 3.3 collective-permute-start.15
  539.2 42.1 %collective-permute-done.12 = f32[512,1216]{0,1:T(8,128)S(1)} collective-permute-done((f32[512,1216]{0,1:T(8,128)S(1)}, f32[512,1216]{0,1:T(8,128)S(1)}, u32[]{:S(2)}, u32[]{:S(2)}) %collective-permute-start.12) | collective-permute-done | bytes 2490400 | tf_op jit(solution)/shard_map/ppermute | solution.py:10
  583.2 6.1 collective-permute-done.15
  592.3 18.8 %collective-permute-done.13 = f32[256,1216]{0,1:T(8,128)S(1)} collective-permute-done((f32[256,1216]{0,1:T(8,128)S(1)}, f32[256,1216]{0,1:T(8,128)S(1)}, u32[]{:S(2)}, u32[]{:S(2)}) %collective-permute-start.13) | collective-permute-done | bytes 1245216 | tf_op jit(solution)/shard_map/ppermute | solution.py:10
  613.5 3.7 collective-permute-start.17
  617.1 4.6 collective-permute-done.14
  622.0 3.4 collective-permute-done.17
  (387 shorter events, 396.7 us)
Async XLA Ops:
  3.1 5.9 copy-start.8
  3.3 5.9 copy-start.10
  3.5 6.1 copy-start.1
  4.8 18.3 %collective-permute-start.3 = (bf16[2,128,1216]{1,2,0:T(8,128)(2,1)}, bf16[2,128,1216]{1,2,0:T(8,128)(2,1)}, u32[]{:S(2)}, u32[]{:S(2)}) collective-permute-start(bf16[2,128,1216]{1,2,0:T(8,128)(2,1)} %pad_maximum_fusion.3), channel_id=1, source_target_pairs={{0,16},{2,18},{4,20},{6,22},{8,24},{10,26},{12,28},{14,30},{16,0},... | collective-permute-start | bytes 1867784 | tf_op jit(solution)/shard_map/ppermute | solution.py:10
  8.9 14.1 %copy-start.3 = (bf16[1,8,1216]{1,2,0:T(8,128)(2,1)}, bf16[1,8,1216]{1,2,0:T(8,128)(2,1)S(1)}, u32[]{:S(2)}) copy-start(bf16[1,8,1216]{1,2,0:T(8,128)(2,1)S(1)} %copy.73) | copy-start | bytes 58372
  9.2 13.9 %copy-start.5 = (bf16[120,1216]{0,1:T(8,128)(2,1)}, bf16[120,1216]{0,1:T(8,128)(2,1)S(1)}, u32[]{:S(2)}) copy-start(bf16[120,1216]{0,1:T(8,128)(2,1)S(1)} %copy.41) | copy-start | bytes 875524
  9.4 16.5 %copy-start.6 = (bf16[8,1216]{0,1:T(8,128)(2,1)}, bf16[8,1216]{0,1:T(8,128)(2,1)S(1)}, u32[]{:S(2)}) copy-start(bf16[8,1216]{0,1:T(8,128)(2,1)S(1)} %copy.42) | copy-start | bytes 58372
  9.6 13.4 %copy-start.4 = (bf16[1,120,1216]{1,2,0:T(8,128)(2,1)}, bf16[1,120,1216]{1,2,0:T(8,128)(2,1)S(1)}, u32[]{:S(2)}) copy-start(bf16[1,120,1216]{1,2,0:T(8,128)(2,1)S(1)} %copy.72) | copy-start | bytes 875524
  10.0 0.7 copy-start.7
  11.6 15.9 %collective-permute-start = (bf16[2,128,1216]{1,2,0:T(8,128)(2,1)}, bf16[2,128,1216]{1,2,0:T(8,128)(2,1)}, u32[]{:S(2)}, u32[]{:S(2)}) collective-permute-start(bf16[2,128,1216]{1,2,0:T(8,128)(2,1)} %pad_maximum_fusion.2), channel_id=1, source_target_pairs={{0,2},{2,0},{4,6},{6,4},{8,10},{10,8},{12,14},{14,12},{16,18},{18,... | collective-permute-start | bytes 1867784 | tf_op jit(solution)/shard_map/ppermute | solution.py:10
  25.9 28.8 %collective-permute-start.4 = (bf16[2,256,1216]{1,2,0:T(8,128)(2,1)}, bf16[2,256,1216]{1,2,0:T(8,128)(2,1)S(1)}, u32[]{:S(2)}, u32[]{:S(2)}) collective-permute-start(bf16[2,256,1216]{1,2,0:T(8,128)(2,1)} %maximum_select_fusion.8), channel_id=1, source_target_pairs={{0,32},{2,34},{4,36},{6,38},{8,40},{10,42},{12,44},{14,46},{16,48}... | collective-permute-start | bytes 3735560 | tf_op jit(solution)/shard_map/ppermute | solution.py:10
  30.3 30.9 %collective-permute-start.1 = (bf16[2,256,1216]{1,2,0:T(8,128)(2,1)}, bf16[2,256,1216]{1,2,0:T(8,128)(2,1)S(1)}, u32[]{:S(2)}, u32[]{:S(2)}) collective-permute-start(bf16[2,256,1216]{1,2,0:T(8,128)(2,1)} %maximum_select_fusion.6), channel_id=1, source_target_pairs={{0,4},{2,6},{4,0},{6,2},{8,12},{10,14},{12,8},{14,10},{16,20},{18,... | collective-permute-start | bytes 3735560 | tf_op jit(solution)/shard_map/ppermute | solution.py:10
  58.1 56.1 %collective-permute-start.5 = (bf16[2,512,1216]{1,2,0:T(8,128)(2,1)}, bf16[2,512,1216]{1,2,0:T(8,128)(2,1)}, u32[]{:S(2)}, u32[]{:S(2)}) collective-permute-start(bf16[2,512,1216]{1,2,0:T(8,128)(2,1)} %maximum_select_fusion.4), channel_id=1, source_target_pairs={{0,64},{2,66},{4,68},{6,70},{8,72},{10,74},{12,76},{14,78},{16,80}... | collective-permute-start | bytes 7471112 | tf_op jit(solution)/shard_map/ppermute | solution.py:10
  64.7 55.9 %collective-permute-start.2 = (bf16[2,512,1216]{1,2,0:T(8,128)(2,1)}, bf16[2,512,1216]{1,2,0:T(8,128)(2,1)}, u32[]{:S(2)}, u32[]{:S(2)}) collective-permute-start(bf16[2,512,1216]{1,2,0:T(8,128)(2,1)} %maximum_select_fusion.2), channel_id=1, source_target_pairs={{0,8},{2,10},{4,12},{6,14},{8,0},{10,2},{12,4},{14,6},{16,24},{18,... | collective-permute-start | bytes 7471112 | tf_op jit(solution)/shard_map/ppermute | solution.py:10
  65.7 4.6 copy-start.2
  133.5 5.7 copy-start.9
  193.5 5.7 collective-permute-start.6
  199.4 7.3 %collective-permute-start.7 = (f32[2,19,1024]{2,1,0:T(8,128)S(1)}, f32[2,19,1024]{2,1,0:T(8,128)S(1)}, u32[]{:S(2)}, u32[]{:S(2)}) collective-permute-start(f32[2,19,1024]{2,1,0:T(8,128)S(1)} %pad_maximum_fusion.5), channel_id=1, source_target_pairs={{0,4},{2,6},{4,0},{6,2},{8,12},{10,14},{12,8},{14,10},{16,20},{18,... | collective-permute-start | bytes 466952 | tf_op jit(solution)/shard_map/ppermute | solution.py:10
  206.7 10.7 %collective-permute-start.8 = (f32[2,19,1024]{2,1,0:T(8,128)S(1)}, f32[2,19,1024]{2,1,0:T(8,128)S(1)}, u32[]{:S(2)}, u32[]{:S(2)}) collective-permute-start(f32[2,19,1024]{2,1,0:T(8,128)S(1)} %pad_maximum_fusion.6), channel_id=1, source_target_pairs={{0,8},{2,10},{4,12},{6,14},{8,0},{10,2},{12,4},{14,6},{16,24},{18,... | collective-permute-start | bytes 466952 | tf_op jit(solution)/shard_map/ppermute | solution.py:10
  295.7 4.7 collective-permute-start.9
  300.4 6.8 %collective-permute-start.10 = (f32[19,1024]{1,0:T(8,128)S(1)}, f32[19,1024]{1,0:T(8,128)S(1)}, u32[]{:S(2)}, u32[]{:S(2)}) collective-permute-start(f32[19,1024]{1,0:T(8,128)S(1)} %add.84), channel_id=1, source_target_pairs={{0,4},{2,6},{4,0},{6,2},{8,12},{10,14},{12,8},{14,10},{16,20},{18,... | collective-permute-start | bytes 233480 | tf_op jit(solution)/shard_map/ppermute | solution.py:10
  307.3 4.9 collective-permute-start.11
  529.6 4.5 slice-start
  529.6 4.5 slice-start.1
  529.6 5.4 copy-start
  532.9 48.5 %collective-permute-start.12 = (f32[512,1216]{0,1:T(8,128)S(1)}, f32[512,1216]{0,1:T(8,128)S(1)}, u32[]{:S(2)}, u32[]{:S(2)}) collective-permute-start(f32[512,1216]{0,1:T(8,128)S(1)} %bitcast.202), channel_id=1, source_target_pairs={{0,8},{2,10},{4,12},{6,14},{8,0},{10,2},{12,4},{14,6},{16,24},{18,... | collective-permute-start | bytes 7471112 | tf_op jit(solution)/shard_map/ppermute | solution.py:10
  535.9 53.4 %collective-permute-start.15 = (bf16[2,512,1216]{1,2,0:T(8,128)(2,1)S(1)}, bf16[2,512,1216]{1,2,0:T(8,128)(2,1)S(1)}, u32[]{:S(2)}, u32[]{:S(2)}) collective-permute-start(bf16[2,512,1216]{1,2,0:T(8,128)(2,1)S(1)} %select_convert_fusion), channel_id=1, source_target_pairs={{0,64},{2,66},{4,68},{6,70},{8,72},{10,74},{12,76},{14,78},{16,80}... | collective-permute-start | bytes 7471112 | tf_op jit(solution)/shard_map/ppermute | solution.py:10
  582.1 29.0 %collective-permute-start.13 = (f32[256,1216]{0,1:T(8,128)S(1)}, f32[256,1216]{0,1:T(8,128)S(1)}, u32[]{:S(2)}, u32[]{:S(2)}) collective-permute-start(f32[256,1216]{0,1:T(8,128)S(1)} %slice_select_fusion.2), channel_id=1, source_target_pairs={{0,4},{2,6},{4,0},{6,2},{8,12},{10,14},{12,8},{14,10},{16,20},{18,... | collective-permute-start | bytes 3735560 | tf_op jit(solution)/shard_map/ppermute | solution.py:10
  590.9 22.0 %collective-permute-start.16 = (bf16[2,256,1216]{1,2,0:T(8,128)(2,1)S(1)}, bf16[2,256,1216]{1,2,0:T(8,128)(2,1)S(1)}, u32[]{:S(2)}, u32[]{:S(2)}) collective-permute-start(bf16[2,256,1216]{1,2,0:T(8,128)(2,1)S(1)} %select_convert_fusion.1), channel_id=1, source_target_pairs={{0,32},{2,34},{4,36},{6,38},{8,40},{10,42},{12,44},{14,46},{16,48}... | collective-permute-start | bytes 3735560 | tf_op jit(solution)/shard_map/ppermute | solution.py:10
  611.4 10.3 %collective-permute-start.14 = (f32[128,1216]{0,1:T(8,128)S(1)}, f32[128,1216]{0,1:T(8,128)S(1)}, u32[]{:S(2)}, u32[]{:S(2)}) collective-permute-start(f32[128,1216]{0,1:T(8,128)S(1)} %slice_select_fusion.3), channel_id=1, source_target_pairs={{0,2},{2,0},{4,6},{6,4},{8,10},{10,8},{12,14},{14,12},{16,18},{18,... | collective-permute-start | bytes 1867784 | tf_op jit(solution)/shard_map/ppermute | solution.py:10
  613.5 11.9 %collective-permute-start.17 = (bf16[2,128,1216]{1,2,0:T(8,128)(2,1)S(1)}, bf16[2,128,1216]{1,2,0:T(8,128)(2,1)S(1)}, u32[]{:S(2)}, u32[]{:S(2)}) collective-permute-start(bf16[2,128,1216]{1,2,0:T(8,128)(2,1)S(1)} %select_convert_fusion.2), channel_id=1, source_target_pairs={{0,16},{2,18},{4,20},{6,22},{8,24},{10,26},{12,28},{14,30},{16,0},... | collective-permute-start | bytes 1867784 | tf_op jit(solution)/shard_map/ppermute | solution.py:10
where the time goes:
time: 633 us; the launch traced here: 628 us
  matrix products  325 us (51%)
  waiting for transfers between devices  164 us (26%)
  other arithmetic  57.8 us (9%)
  local copies, waits for them, and re-layouts  38.8 us (6%)
  starting transfers between devices  38.6 us (6%)
    ppermute x18, waiting for transfers between devices, partner_2(): lax.ppermute(x, axis, [(i, i ^ 1 << stride) for i in range(lax.axis_size(...  164 us
    dot_general x57, matrix products, scores_of(): jnp.einsum('qd,kd->qk', query, key_h, preferred_element_type=jnp.float32)  99.4 us
    dot_general x38, matrix products, dprobs_of(): jnp.einsum('qd,kd->qk', grad, value, preferred_element_type=jnp.float32)  87.5 us
    dot_general x19, matrix products, gradients(): jnp.einsum('qk,qd->kd', probs.astype(jnp.bfloat16), grad, preferred_eleme...  51 us
    dot_general x19, matrix products, gradients(): jnp.einsum('qk,kd->qd', dscore, key_h, preferred_element_type=jnp.float32)  46 us
    dot_general x19, matrix products, gradients(): jnp.einsum('qk,qd->kd', dscore, query, preferred_element_type=jnp.float32)  41.4 us
    ppermute x18, starting transfers between devices, partner_2(): lax.ppermute(x, axis, [(i, i ^ 1 << stride) for i in range(lax.axis_size(...  38.6 us
    while x4, local copies, waits for them, and re-layouts, body(): grad_q, grad_k, grad_v = lax.map(gradients, operands + (lse, delta))  21.2 us
  transfers between devices with their start and end apart: 18, of which 14 were waited for; matrix products, arithmetic and copies ran while one was open for 7% of the time, Pallas kernels for 0%

commit v1 on v0

v1 whole, which is shorter than its diff:
```python
import jax
import jax.numpy as jnp
from jax import lax
from jax.experimental import pallas as pl
from jax.experimental.pallas import tpu as pltpu
from jax.sharding import PartitionSpec as P

F32 = jnp.float32
BF = jnp.bfloat16
MESH = pl.DeviceIdType.MESH
NT = (((1,), (1,)), ((), ()))
NN = (((1,), (0,)), ((), ()))
HEAD_DIM = 64
SIDE = 4
HG = 5
TOK = 128
ROWS = SIDE * TOK
KEYS = SIDE * ROWS
SCALE = HEAD_DIM**-0.5
LOG = SCALE * 1.4426950408889634
NEG = -1e30
CHUNK = 256


def dot(a, b, dims):
    return lax.dot_general(a, b, dims, preferred_element_type=F32)


def kernel(
    tl_ref, qg_own, kv_own, out_ref,
    qg_all, kv_all, kt_all, s_ref, p_ref, dp_ref, ak, av, st,
    dq_st, dkv_st, rs_q, rs_kv, g_q, g_kv, f_q, f_kv,
    a_s, a_r, b_s, b_r, st_s, st_r, r_s, r_r, g_s, g_r,
):
    seq = lax.axis_index("seq")
    core = lax.axis_index("head")
    y, z, x = seq // 16, lax.rem(seq // 4, 4), lax.rem(seq, 4)

    def fwd(i, r):
        return lax.rem(i + r, SIDE)

    def back(i, r):
        return lax.rem(i + SIDE - r, SIDE)

    def at_x(i):
        return (y * 16 + z * 4 + i, core)

    def at_y(i):
        return (i * 16 + z * 4 + x, core)

    def at_z(i):
        return (y * 16 + i * 4 + x, core)

    def remote(src, dst, send, recv, device):
        return pltpu.make_async_remote_copy(
            src_ref=src, dst_ref=dst, send_sem=send, recv_sem=recv,
            device_id=device, device_id_type=MESH,
        )

    others = range(1, SIDE)

    def copies_a(h, r):
        t = fwd(x, r)
        return [
            remote(qg_own.at[HG * t + h], qg_all.at[h, y, x], a_s.at[0, h, r], a_r.at[0, h, r], at_x(t)),
            remote(kv_own.at[HG * t + h], kv_all.at[h, z, x], a_s.at[1, h, r], a_r.at[1, h, r], at_x(t)),
        ]

    def arrive_a(h, r):
        f = back(x, r)
        return [
            remote(qg_own.at[h], qg_all.at[h, y, f], a_s.at[0, h, r], a_r.at[0, h, r], at_x(f)),
            remote(kv_own.at[h], kv_all.at[h, z, f], a_s.at[1, h, r], a_r.at[1, h, r], at_x(f)),
        ]

    def copies_b(h, r):
        return [
            remote(qg_all.at[h, y], qg_all.at[h, y], b_s.at[0, h, r], b_r.at[0, h, r], at_y(fwd(y, r))),
            remote(kv_all.at[h, z], kv_all.at[h, z], b_s.at[1, h, r], b_r.at[1, h, r], at_z(fwd(z, r))),
        ]

    def arrive_b(h, r):
        fy, fz = back(y, r), back(z, r)
        return [
            remote(qg_all.at[h, fy], qg_all.at[h, fy], b_s.at[0, h, r], b_r.at[0, h, r], at_y(fy)),
            remote(kv_all.at[h, fz], kv_all.at[h, fz], b_s.at[1, h, r], b_r.at[1, h, r], at_z(fz)),
        ]

    def copy_st(u, r):
        return remote(st.at[u, 0], st.at[u, r], st_s.at[u, r], st_r.at[u, r], at_y(fwd(y, r)))

    def copy_rq(h, r):
        t = fwd(y, r)
        return remote(dq_st.at[h, t], rs_q.at[h, r - 1], r_s.at[0, h, r], r_r.at[0, h, r], at_y(t))

    def copy_rkv(h, r):
        t = fwd(z, r)
        return remote(dkv_st.at[h, t], rs_kv.at[h, r - 1], r_s.at[1, h, r], r_r.at[1, h, r], at_z(t))

    def copies_g(h, r):
        t = fwd(x, r)
        return [
            remote(g_q.at[h, t], f_q.at[HG * x + h], g_s.at[0, h, r], g_r.at[0, h, r], at_x(t)),
            remote(g_kv.at[h, t], f_kv.at[HG * x + h], g_s.at[1, h, r], g_r.at[1, h, r], at_x(t)),
        ]

    def arrive_g(h, r):
        f = back(x, r)
        return [
            remote(g_q.at[h, f], f_q.at[HG * f + h], g_s.at[0, h, r], g_r.at[0, h, r], at_x(f)),
            remote(g_kv.at[h, f], f_kv.at[HG * f + h], g_s.at[1, h, r], g_r.at[1, h, r], at_x(f)),
        ]

    barrier = pltpu.get_barrier_semaphore()
    for r in others:
        for place in (at_x(fwd(x, r)), at_y(fwd(y, r)), at_z(fwd(z, r))):
            pl.semaphore_signal(barrier, inc=1, device_id=place, device_id_type=MESH)
    pl.semaphore_wait(barrier, 3 * (SIDE - 1))

    def start_a(h, carry):
        for r in others:
            for copy in copies_a(h, r):
                copy.start()
        qg_all[h, y, x] = qg_own[HG * x + h]
        kv_all[h, z, x] = kv_own[HG * x + h]
        return carry

    lax.fori_loop(0, HG, start_a, 0)

    def spread(h):
        for r in others:
            for copy in arrive_a(h, r):
                copy.wait_recv()
        for r in others:
            for copy in copies_b(h, r):
                copy.start()

    def receive(h):
        for r in others:
            for copy in arrive_b(h, r):
                copy.wait_recv()
        for k in range(SIDE):
            kt_all[h, k] = kv_all[h, k].reshape(ROWS, TOK).T[:HEAD_DIM]

    def phase1(h, half):
        def block(j, carry):
            qg = qg_all[h, 2 * half + j].reshape(ROWS, TOK)
            lane = lax.broadcasted_iota(jnp.int32, qg.shape, 1)
            q0 = jnp.where(lane < HEAD_DIM, qg, jnp.zeros_like(qg))
            g0 = jnp.where(lane < HEAD_DIM, jnp.zeros_like(qg), qg)
            sub = lax.broadcasted_iota(jnp.int32, (8, ROWS), 0)
            top = jnp.full((8, ROWS), NEG, F32)
            for k in range(SIDE):
                s = dot(kv_all[h, k].reshape(ROWS, TOK), q0, NT)
                s_ref[k * ROWS : (k + 1) * ROWS, :] = s
                parts = s.reshape(SIDE, TOK // 8, 8, ROWS)
                top = jnp.maximum(top, jnp.max(parts[:, : TOK // 8 - 1].reshape(-1, 8, ROWS), axis=0))
                for i in range(SIDE):
                    valid = (y * 16 + k * 4 + i) * 8 + sub < tl_ref[0]
                    text = jnp.where(valid, parts[i, TOK // 8 - 1], NEG)
                    end = k * ROWS + (i + 1) * TOK
                    s_ref[end - 8 : end, :] = text
                    top = jnp.maximum(top, text)
            top = jnp.max(top, axis=0, keepdims=True) * LOG
            total = jnp.zeros((8, ROWS), F32)
            weighted = jnp.zeros((8, ROWS), F32)
            for k in range(SIDE):
                rows = slice(k * ROWS, (k + 1) * ROWS)
                d = dot(kv_all[h, k].reshape(ROWS, TOK), g0, NT)
                p = jnp.exp2(s_ref[rows, :] * LOG - top)
                total += jnp.sum(p.reshape(-1, 8, ROWS), axis=0)
                weighted += jnp.sum((p * d).reshape(-1, 8, ROWS), axis=0)
                p_ref[half, j, rows, :] = p.astype(BF)
                dp_ref[half, j, rows, :] = d
            st[2 * h + half, 0, j] = jnp.concatenate(
                [
                    top,
                    jnp.sum(total, axis=0, keepdims=True),
                    jnp.sum(weighted, axis=0, keepdims=True),
                    jnp.zeros((5, ROWS), F32),
                ],
                0,
            )
            return carry

        lax.fori_loop(0, 2, block, 0)
        for r in others:
            copy_st(2 * h + half, r).start()

    def phase2(h, half):
        u = 2 * h + half
        for r in others:
            copy_st(u, r).wait_recv()
        if half == 0:
            ak[...] = jnp.zeros_like(ak)
            av[...] = jnp.zeros_like(av)

        def block(j, carry):
            stats = [st[u, r, j] for r in range(SIDE)]
            tops = [s[0:1] for s in stats]
            top = jnp.maximum(jnp.maximum(tops[0], tops[1]), jnp.maximum(tops[2], tops[3]))
            parts = [jnp.exp2(t - top) for t in tops]
            total = sum(s[1:2] * e for s, e in zip(stats, parts))
            factor = parts[0] / total
            delta = sum(s[2:3] * e for s, e in zip(stats, parts)) / total
            qg = qg_all[h, 2 * half + j].reshape(ROWS, TOK)
            dq = jnp.zeros((HEAD_DIM, ROWS), F32)
            for c in range(KEYS // CHUNK):
                rows = slice(c * CHUNK, (c + 1) * CHUNK)
                p = p_ref[half, j, rows, :].astype(F32) * factor
                ds = (p * (dp_ref[half, j, rows, :] - delta)).astype(BF)
                av[rows, :] += dot(p.astype(BF), qg, NN)
                ak[rows, :] += dot(ds, qg, NN)
                per = ROWS // CHUNK
                part = c % per * CHUNK
                dq += dot(kt_all[h, c // per, :, part : part + CHUNK], ds, NN)
            dq_st[h, 2 * half + j] = (dq * SCALE).astype(BF)
            return carry

        lax.fori_loop(0, 2, block, 0)
        for r in others:
            t = fwd(y, r)

            @pl.when(t // 2 == half)
            def _():
                copy_rq(h, r).start()

        if half == 1:
            lane = lax.broadcasted_iota(jnp.int32, (ROWS, TOK), 1)
            for k in range(SIDE):
                rows = slice(k * ROWS, (k + 1) * ROWS)
                dkv_st[h, k] = jnp.where(lane < HEAD_DIM, ak[rows, :] * SCALE, av[rows, :]).astype(BF)
            for r in others:
                copy_rkv(h, r).start()

    def hand_over(h):
        for r in others:
            copy_rq(h, r).wait_recv()
            copy_rkv(h, r).wait_recv()
        dq = dq_st[h, y].astype(F32)
        dkv = dkv_st[h, z].astype(F32)
        for r in others:
            dq += rs_q[h, r - 1].astype(F32)
            dkv += rs_kv[h, r - 1].astype(F32)
        for i in range(SIDE):
            g_q[h, i] = dq[:, i * TOK : (i + 1) * TOK].astype(BF)
            g_kv[h, i] = dkv[i * TOK : (i + 1) * TOK, :].astype(BF)
        for r in others:
            for copy in copies_g(h, r):
                copy.start()
        f_q[HG * x + h] = g_q[h, x]
        f_kv[HG * x + h] = g_kv[h, x]

    spread(0)

    def step(h, carry):
        @pl.when(h < HG)
        def _():
            receive(h)
            phase1(h, 0)

        @pl.when(h < HG - 1)
        def _():
            spread(h + 1)

        @pl.when(h > 0)
        def _():
            phase2(h - 1, 1)

        @pl.when(h < HG)
        def _():
            phase1(h, 1)
            phase2(h, 0)

        @pl.when(h > 0)
        def _():
            hand_over(h - 1)

        return carry

    lax.fori_loop(0, HG + 1, step, 0)

    def finish(h, carry):
        for r in others:
            for copy in arrive_g(h, r):
                copy.wait_recv()
            for copy in copies_a(h, r) + copies_b(h, r) + copies_g(h, r):
                copy.wait_send()
            copy_rq(h, r).wait_send()
            copy_rkv(h, r).wait_send()
            copy_st(2 * h, r).wait_send()
            copy_st(2 * h + 1, r).wait_send()
        return carry

    lax.fori_loop(0, HG, finish, 0)

    for pair in range(SIDE * HG // 2):
        cols = slice(pair * TOK, (pair + 1) * TOK)
        first, second = f_kv[2 * pair].astype(F32), f_kv[2 * pair + 1].astype(F32)
        query = jnp.concatenate([f_q[2 * pair], f_q[2 * pair + 1]], 0).astype(F32)
        out_ref[0, :, cols] = query.T.astype(BF)
        out_ref[1, :, cols] = jnp.concatenate([first[:, :HEAD_DIM], second[:, :HEAD_DIM]], 1).astype(BF)
        out_ref[2, :, cols] = jnp.concatenate([first[:, HEAD_DIM:], second[:, HEAD_DIM:]], 1).astype(BF)


def body(image_qkv, text_qkv, image_grad, text_grad, text_len):
    image_rows = image_qkv.shape[1]
    width = image_qkv.shape[2]
    heads = width // HEAD_DIM
    slots = SIDE * HG

    def per_head(image, text):
        whole = jnp.concatenate([image, text], 0).reshape(TOK, heads, HEAD_DIM)
        return jnp.moveaxis(whole, 1, 0)

    query, key, value = (per_head(image_qkv[i], text_qkv[i]) for i in range(3))
    grad = per_head(image_grad, text_grad)
    pad = ((0, slots - heads), (0, 0), (0, 0))
    qg = jnp.pad(jnp.concatenate([query, grad], -1), pad)
    kv = jnp.pad(jnp.concatenate([key, value], -1), pad)
    vmem = pl.BlockSpec(memory_space=pltpu.VMEM)
    out = pl.pallas_call(
        kernel,
        out_shape=jax.ShapeDtypeStruct((3, TOK, slots * HEAD_DIM), BF),
        in_specs=[pl.BlockSpec(memory_space=pltpu.SMEM), vmem, vmem],
        out_specs=vmem,
        scratch_shapes=[
            pltpu.VMEM((HG, SIDE, SIDE, TOK, TOK), BF),
            pltpu.VMEM((HG, SIDE, SIDE, TOK, TOK), BF),
            pltpu.VMEM((HG, SIDE, HEAD_DIM, ROWS), BF),
            pltpu.VMEM((KEYS, ROWS), F32),
            pltpu.VMEM((2, 2, KEYS, ROWS), BF),
            pltpu.VMEM((2, 2, KEYS, ROWS), F32),
            pltpu.VMEM((KEYS, TOK), F32),
            pltpu.VMEM((KEYS, TOK), F32),
            pltpu.VMEM((2 * HG, SIDE, 2, 8, ROWS), F32),
            pltpu.VMEM((HG, SIDE, HEAD_DIM, ROWS), BF),
            pltpu.VMEM((HG, SIDE, ROWS, TOK), BF),
            pltpu.VMEM((HG, SIDE - 1, HEAD_DIM, ROWS), BF),
            pltpu.VMEM((HG, SIDE - 1, ROWS, TOK), BF),
            pltpu.VMEM((HG, SIDE, HEAD_DIM, TOK), BF),
            pltpu.VMEM((HG, SIDE, TOK, TOK), BF),
            pltpu.VMEM((slots, HEAD_DIM, TOK), BF),
            pltpu.VMEM((slots, TOK, TOK), BF),
        ]
        + [
            pltpu.SemaphoreType.DMA(shape)
            for shape in [(2, HG, SIDE)] * 4 + [(2 * HG, SIDE)] * 2 + [(2, HG, SIDE)] * 4
        ],
        compiler_params=pltpu.CompilerParams(
            collective_id=0, has_side_effects=True, vmem_limit_bytes=60 * 2**20
        ),
    )(text_len, qg, kv)
    return (out[:, :image_rows, :width], out[:, image_rows:, :width])


def solution(mesh):
    return jax.shard_map(
        body,
        mesh=mesh,
        in_specs=(
            P(None, "seq", "head"),
            P(None, "seq", "head"),
            P("seq", "head"),
            P("seq", "head"),
            P(),
        ),
        out_specs=(P(None, "seq", "head"), P(None, "seq", "head")),
        check_vma=False,
    )
```

time: 633 us -> 129 us (0.20)
  matrix products: 325 us -> 0 us
  waiting for transfers between devices: 164 us -> 0 us
  Pallas kernels: 0 us -> 116 us
  other arithmetic: 57.8 us -> 3.1 us
  starting transfers between devices: 38.6 us -> 0 us
  local copies, waits for them, and re-layouts: 38.8 us -> 7.89 us
    dot_general x152 -> x0, matrix products: 325 us -> none  [the longest x57 99.4 us: scores_of(): jnp.einsum('qd,kd->qk', query, key_h, preferred_element_type=jnp.float32)]
    ppermute x18 -> x0, waiting for transfers between devices: 164 us -> none  [partner_2(): lax.ppermute(x, axis, [(i, i ^ 1 << stride) for i in range(lax.axis_size(...]
    pallas_call x0 -> x1, Pallas kernels: none -> 116 us  [body(): pl.pallas_call(kernel, out_shape=jax.ShapeDtypeStruct((3, TOK, slots * HE...]
    ppermute x18 -> x0, starting transfers between devices: 38.6 us -> none  [partner_2(): lax.ppermute(x, axis, [(i, i ^ 1 << stride) for i in range(lax.axis_size(...]
    select_n x11 -> x0, other arithmetic: 22.7 us -> none  [the longest x8 19.2 us: gather_bits(): jnp.where(upper, jnp.concatenate([partner, block], 1), jnp.concatenate([b...]
    while x4 -> x0, local copies, waits for them, and re-layouts: 21.2 us -> none  [body(): grad_q, grad_k, grad_v = lax.map(gradients, operands + (lse, delta))]
    reduce_sum x19 -> x0, other arithmetic: 17.2 us -> none  [max_sum(): return jnp.stack([top, jnp.sum(jnp.exp(scores - top[:, None]), 1)])]
    transpose x2, other arithmetic: 8.67 us -> 0.52 us  [per_head(): return jnp.moveaxis(whole, 1, 0)]
  transfers between devices with their start and end apart: 18 -> 0, of which waited for: 14 -> 0; matrix products, arithmetic and copies ran while one was open for 7% -> 0% of each run, Pallas kernels for 0% -> 0%
where the time goes in v1:
time: 129 us; the launch traced here: 128 us
  Pallas kernels  116 us (90%)
  local copies, waits for them, and re-layouts  7.89 us (6%)
  other arithmetic  3.1 us (2%)
  between operations  1.42 us (1%)
    pallas_call x1, Pallas kernels, body(): pl.pallas_call(kernel, out_shape=jax.ShapeDtypeStruct((3, TOK, slots * HE...  116 us
    slice x2, local copies, waits for them, and re-layouts, body(): return (out[:, :image_rows, :width], out[:, image_rows:, :width])  3.63 us

profile of v1, /device:TPU:0, one launch (start us, length us, event | category | flops | bytes accessed | tf_op | source)
XLA Modules:
  0.0 128.3 jit_solution(448196124000361888)
XLA Ops:
  0.6 1.2 fusion.6
  1.8 0.2 copy.20
  2.1 0.0 copy-start.1
  2.1 0.3 copy.14
  2.4 0.2 copy.21
  2.6 0.3 copy.17
  2.9 0.0 copy-done.1
  3.0 0.1 concatenate.39
  3.1 0.1 concatenate.42
  3.2 0.4 maximum_bitcast_fusion.1
  3.6 1.2 fusion.5.kv_own
  4.8 0.2 copy.19
  5.0 0.0 copy-start
  5.0 0.3 copy.8
  5.3 0.1 concatenate.34
  5.4 0.0 copy-start.2
  5.4 0.2 maximum_bitcast_fusion
  5.6 0.4 copy-done
  6.0 0.2 copy.10
  6.2 0.0 copy-done.2
  6.2 0.2 copy.11
  6.4 0.2 pad_maximum_fusion
  6.6 0.3 copy.12
  6.9 1.2 fusion.4.qg_own
  8.8 115.9 %shard_map.68 = bf16[3,128,1280]{2,1,0:T(8,128)(2,1)} custom-call(s32[1]{0:T(128)S(6)} %copy.22.tl_ref, bf16[20,128,128]{2,1,0:T(8,128)(2,1)} %fusion.4.qg_own, bf16[20,128,128]{2,1,0:T(8,128)(2,1)} %fusion.5.kv_own), custom_call_target="tpu_custom_call" | custom-call | tf_op jit(solution)/shard_map/pallas_call | solution.py:322
  124.7 2.2 %slice.30 = bf16[3,120,1216]{2,1,0:T(8,128)(2,1)} slice(bf16[3,128,1280]{2,1,0:T(8,128)(2,1)} %shard_map.68), slice={[0:3], [0:120], [0:1216]} | slice | bytes 1751040 | tf_op jit(solution)/shard_map/slice | solution.py:354
  126.8 1.5 %slice.31 = bf16[3,8,1216]{2,1,0:T(8,128)(2,1)} slice(bf16[3,128,1280]{2,1,0:T(8,128)(2,1)} %shard_map.68), slice={[0:3], [120:128], [0:1216]} | slice | bytes 116736 | tf_op jit(solution)/shard_map/slice | solution.py:354
  (4 shorter events, 0.0 us)
Async XLA Ops:
  2.1 0.9 copy-start.1
  5.0 1.0 copy-start
  5.4 0.8 copy-start.2

commit v2 on v1

--- a/solution.py
+++ b/solution.py
@@ -27,9 +27,9 @@
 
 
 def kernel(
-    tl_ref, qg_own, kv_own, out_ref,
-    qg_all, kv_all, kt_all, s_ref, p_ref, dp_ref, ak, av, st,
-    dq_st, dkv_st, rs_q, rs_kv, g_q, g_kv, f_q, f_kv,
+    tl_ref, image_qkv, text_qkv, image_grad, text_grad, image_out, text_out,
+    qg_own, kv_own, qg_all, kv_all, kt_all, s_ref, p_ref, dp_ref, ak, av, st,
+    dq_st, dkv_st, r1_q, r1_kv, r2_q, r2_kv, g_q, g_kv, f_q, f_kv,
     a_s, a_r, b_s, b_r, st_s, st_r, r_s, r_r, g_s, g_r,
 ):
     seq = lax.axis_index("seq")
@@ -73,29 +73,62 @@
             remote(kv_own.at[h], kv_all.at[h, z, f], a_s.at[1, h, r], a_r.at[1, h, r], at_x(f)),
         ]
 
-    def copies_b(h, r):
-        return [
-            remote(qg_all.at[h, y], qg_all.at[h, y], b_s.at[0, h, r], b_r.at[0, h, r], at_y(fwd(y, r))),
-            remote(kv_all.at[h, z], kv_all.at[h, z], b_s.at[1, h, r], b_r.at[1, h, r], at_z(fwd(z, r))),
-        ]
-
-    def arrive_b(h, r):
-        fy, fz = back(y, r), back(z, r)
-        return [
-            remote(qg_all.at[h, fy], qg_all.at[h, fy], b_s.at[0, h, r], b_r.at[0, h, r], at_y(fy)),
-            remote(kv_all.at[h, fz], kv_all.at[h, fz], b_s.at[1, h, r], b_r.at[1, h, r], at_z(fz)),
-        ]
+    def copies_b(h):
+        yn, yp, zn, zp = fwd(y, 1), back(y, 1), fwd(z, 1), back(z, 1)
+        return [
+            remote(qg_all.at[h, y], qg_all.at[h, y], b_s.at[0, h, 0], b_r.at[0, h, 0], at_y(yn)),
+            remote(kv_all.at[h, z], kv_all.at[h, z], b_s.at[1, h, 0], b_r.at[1, h, 0], at_z(zn)),
+            remote(qg_all.at[h, y], qg_all.at[h, y], b_s.at[0, h, 1], b_r.at[0, h, 1], at_y(yp)),
+            remote(kv_all.at[h, z], kv_all.at[h, z], b_s.at[1, h, 1], b_r.at[1, h, 1], at_z(zp)),
+        ]
+
+    def arrive_b(h):
+        yn, yp, zn, zp = fwd(y, 1), back(y, 1), fwd(z, 1), back(z, 1)
+        return [
+            remote(qg_all.at[h, yp], qg_all.at[h, yp], b_s.at[0, h, 0], b_r.at[0, h, 0], at_y(yp)),
+            remote(kv_all.at[h, zp], kv_all.at[h, zp], b_s.at[1, h, 0], b_r.at[1, h, 0], at_z(zp)),
+            remote(qg_all.at[h, yn], qg_all.at[h, yn], b_s.at[0, h, 1], b_r.at[0, h, 1], at_y(yn)),
+            remote(kv_all.at[h, zn], kv_all.at[h, zn], b_s.at[1, h, 1], b_r.at[1, h, 1], at_z(zn)),
+        ]
+
+    def relays(h, part, from_y, from_z, to_y, to_z):
+        half = pl.ds(part * 2, 2)
+        q = qg_all.at[h, from_y, half]
+        k = kv_all.at[h, from_z, half]
+        n = 2 + part
+        return [
+            remote(q, q, b_s.at[0, h, n], b_r.at[0, h, n], at_y(to_y)),
+            remote(k, k, b_s.at[1, h, n], b_r.at[1, h, n], at_z(to_z)),
+        ]
+
+    def copies_f(h):
+        yn, yp, zn, zp = fwd(y, 1), back(y, 1), fwd(z, 1), back(z, 1)
+        return relays(h, 0, yp, zp, yn, zn) + relays(h, 1, yn, zn, yp, zp)
+
+    def arrive_f(h):
+        yn, yp, zn, zp = fwd(y, 1), back(y, 1), fwd(z, 1), back(z, 1)
+        yo, zo = fwd(y, 2), fwd(z, 2)
+        return relays(h, 0, yo, zo, yp, zp) + relays(h, 1, yo, zo, yn, zn)
 
     def copy_st(u, r):
         return remote(st.at[u, 0], st.at[u, r], st_s.at[u, r], st_r.at[u, r], at_y(fwd(y, r)))
 
-    def copy_rq(h, r):
-        t = fwd(y, r)
-        return remote(dq_st.at[h, t], rs_q.at[h, r - 1], r_s.at[0, h, r], r_r.at[0, h, r], at_y(t))
-
-    def copy_rkv(h, r):
-        t = fwd(z, r)
-        return remote(dkv_st.at[h, t], rs_kv.at[h, r - 1], r_s.at[1, h, r], r_r.at[1, h, r], at_z(t))
+    def copies_r1(h):
+        yo, zo = fwd(y, 2), fwd(z, 2)
+        places = ((at_y(fwd(y, 1)), at_z(fwd(z, 1))), (at_y(back(y, 1)), at_z(back(z, 1))))
+        copies = []
+        for n, (to_y, to_z) in enumerate(places):
+            copies.append(remote(dq_st.at[h, yo, n], r1_q.at[h, n], r_s.at[0, h, n], r_r.at[0, h, n], to_y))
+            copies.append(remote(dkv_st.at[h, zo, n], r1_kv.at[h, n], r_s.at[1, h, n], r_r.at[1, h, n], to_z))
+        return copies
+
+    def copies_r2(h):
+        copies = []
+        for n, (ty, tz) in enumerate(((fwd(y, 1), fwd(z, 1)), (back(y, 1), back(z, 1)))):
+            k = 2 + n
+            copies.append(remote(dq_st.at[h, ty], r2_q.at[h, n], r_s.at[0, h, k], r_r.at[0, h, k], at_y(ty)))
+            copies.append(remote(dkv_st.at[h, tz], r2_kv.at[h, n], r_s.at[1, h, k], r_r.at[1, h, k], at_z(tz)))
+        return copies
 
     def copies_g(h, r):
         t = fwd(x, r)
@@ -115,30 +148,48 @@
     for r in others:
         for place in (at_x(fwd(x, r)), at_y(fwd(y, r)), at_z(fwd(z, r))):
             pl.semaphore_signal(barrier, inc=1, device_id=place, device_id_type=MESH)
+
+    def column(image, text, pair):
+        cols = slice(pair * TOK, min((pair + 1) * TOK, image.shape[-1]))
+        return jnp.concatenate([image[:, cols].astype(F32), text[:, cols].astype(F32)], 0)
+
+    heads = image_grad.shape[1] // HEAD_DIM
+    for pair in range((heads + 1) // 2):
+        query, key, value = (column(image_qkv.at[i], text_qkv.at[i], pair) for i in range(3))
+        grad = column(image_grad, text_grad, pair)
+        for own, left, right in ((qg_own, query, grad), (kv_own, key, value)):
+            own[2 * pair] = jnp.concatenate([left[:, :HEAD_DIM], right[:, :HEAD_DIM]], 1).astype(BF)
+            if 2 * pair + 1 < heads:
+                own[2 * pair + 1] = jnp.concatenate([left[:, HEAD_DIM:], right[:, HEAD_DIM:]], 1).astype(BF)
+    for slot in range(heads, SIDE * HG):
+        qg_own[slot] = jnp.zeros((TOK, TOK), BF)
+        kv_own[slot] = jnp.zeros((TOK, TOK), BF)
+
     pl.semaphore_wait(barrier, 3 * (SIDE - 1))
 
-    def start_a(h, carry):
+    def start_a(h):
         for r in others:
             for copy in copies_a(h, r):
                 copy.start()
         qg_all[h, y, x] = qg_own[HG * x + h]
         kv_all[h, z, x] = kv_own[HG * x + h]
-        return carry
-
-    lax.fori_loop(0, HG, start_a, 0)
 
     def spread(h):
         for r in others:
             for copy in arrive_a(h, r):
                 copy.wait_recv()
-        for r in others:
-            for copy in copies_b(h, r):
-                copy.start()
+        for copy in copies_b(h):
+            copy.start()
+
+    def forward(h):
+        for copy in arrive_b(h):
+            copy.wait_recv()
+        for copy in copies_f(h):
+            copy.start()
 
     def receive(h):
-        for r in others:
-            for copy in arrive_b(h, r):
-                copy.wait_recv()
+        for copy in arrive_f(h):
+            copy.wait_recv()
         for k in range(SIDE):
             kt_all[h, k] = kv_all[h, k].reshape(ROWS, TOK).T[:HEAD_DIM]
 
@@ -172,15 +223,9 @@
                 weighted += jnp.sum((p * d).reshape(-1, 8, ROWS), axis=0)
                 p_ref[half, j, rows, :] = p.astype(BF)
                 dp_ref[half, j, rows, :] = d
-            st[2 * h + half, 0, j] = jnp.concatenate(
-                [
-                    top,
-                    jnp.sum(total, axis=0, keepdims=True),
-                    jnp.sum(weighted, axis=0, keepdims=True),
-                    jnp.zeros((5, ROWS), F32),
-                ],
-                0,
-            )
+            stats = (top, jnp.sum(total, axis=0, keepdims=True), jnp.sum(weighted, axis=0, keepdims=True))
+            parts = [s[:, i * TOK : (i + 1) * TOK] for s in stats for i in range(SIDE)]
+            st[2 * h + half, 0, j] = jnp.concatenate(parts + [jnp.zeros((SIDE, TOK), F32)], 0)
             return carry
 
         lax.fori_loop(0, 2, block, 0)
@@ -197,12 +242,15 @@
 
         def block(j, carry):
             stats = [st[u, r, j] for r in range(SIDE)]
-            tops = [s[0:1] for s in stats]
+            tops = [s[0:4] for s in stats]
             top = jnp.maximum(jnp.maximum(tops[0], tops[1]), jnp.maximum(tops[2], tops[3]))
             parts = [jnp.exp2(t - top) for t in tops]
-            total = sum(s[1:2] * e for s, e in zip(stats, parts))
+            total = sum(s[4:8] * e for s, e in zip(stats, parts))
             factor = parts[0] / total
-            delta = sum(s[2:3] * e for s, e in zip(stats, parts)) / total
+            delta = sum(s[8:12] * e for s, e in zip(stats, parts)) / total
+            factor, delta = (
+                jnp.concatenate([v[i : i + 1] for i in range(SIDE)], 1) for v in (factor, delta)
+            )
             qg = qg_all[h, 2 * half + j].reshape(ROWS, TOK)
             dq = jnp.zeros((HEAD_DIM, ROWS), F32)
             for c in range(KEYS // CHUNK):
@@ -214,49 +262,61 @@
                 per = ROWS // CHUNK
                 part = c % per * CHUNK
                 dq += dot(kt_all[h, c // per, :, part : part + CHUNK], ds, NN)
-            dq_st[h, 2 * half + j] = (dq * SCALE).astype(BF)
+            dq = (dq * SCALE).astype(BF)
+            for i in range(2):
+                dq_st[h, 2 * half + j, i] = dq[:, i * ROWS // 2 : (i + 1) * ROWS // 2]
             return carry
 
         lax.fori_loop(0, 2, block, 0)
-        for r in others:
-            t = fwd(y, r)
-
-            @pl.when(t // 2 == half)
-            def _():
-                copy_rq(h, r).start()
-
         if half == 1:
             lane = lax.broadcasted_iota(jnp.int32, (ROWS, TOK), 1)
             for k in range(SIDE):
                 rows = slice(k * ROWS, (k + 1) * ROWS)
-                dkv_st[h, k] = jnp.where(lane < HEAD_DIM, ak[rows, :] * SCALE, av[rows, :]).astype(BF)
-            for r in others:
-                copy_rkv(h, r).start()
+                dkv = jnp.where(lane < HEAD_DIM, ak[rows, :] * SCALE, av[rows, :]).astype(BF)
+                dkv_st[h, k] = dkv.reshape(2, ROWS // 2, TOK)
+            for copy in copies_r1(h):
+                copy.start()
+
+    def combine(h):
+        for copy in copies_r1(h):
+            copy.wait_recv()
+        for n, (ty, tz) in enumerate(((fwd(y, 1), fwd(z, 1)), (back(y, 1), back(z, 1)))):
+            dq_st[h, ty, n] = (dq_st[h, ty, n].astype(F32) + r1_q[h, n].astype(F32)).astype(BF)
+            dkv_st[h, tz, n] = (dkv_st[h, tz, n].astype(F32) + r1_kv[h, n].astype(F32)).astype(BF)
+        for copy in copies_r2(h):
+            copy.start()
 
     def hand_over(h):
-        for r in others:
-            copy_rq(h, r).wait_recv()
-            copy_rkv(h, r).wait_recv()
-        dq = dq_st[h, y].astype(F32)
-        dkv = dkv_st[h, z].astype(F32)
-        for r in others:
-            dq += rs_q[h, r - 1].astype(F32)
-            dkv += rs_kv[h, r - 1].astype(F32)
-        for i in range(SIDE):
-            g_q[h, i] = dq[:, i * TOK : (i + 1) * TOK].astype(BF)
-            g_kv[h, i] = dkv[i * TOK : (i + 1) * TOK, :].astype(BF)
+        for copy in copies_r2(h):
+            copy.wait_recv()
+        for i in range(2):
+            dq = dq_st[h, y, i].astype(F32) + r2_q[h, 0, i].astype(F32) + r2_q[h, 1, i].astype(F32)
+            dkv = dkv_st[h, z, i].astype(F32) + r2_kv[h, 0, i].astype(F32) + r2_kv[h, 1, i].astype(F32)
+            for k in range(2):
+                g_q[h, 2 * i + k] = dq[:, k * TOK : (k + 1) * TOK].astype(BF)
+                g_kv[h, 2 * i + k] = dkv[k * TOK : (k + 1) * TOK, :].astype(BF)
         for r in others:
             for copy in copies_g(h, r):
                 copy.start()
         f_q[HG * x + h] = g_q[h, x]
         f_kv[HG * x + h] = g_kv[h, x]
 
+    start_a(0)
     spread(0)
+    start_a(1)
+    forward(0)
 
     def step(h, carry):
         @pl.when(h < HG)
         def _():
             receive(h)
+
+        @pl.when(h < HG - 2)
+        def _():
+            start_a(h + 2)
+
+        @pl.when(h < HG)
+        def _():
             phase1(h, 0)
 
         @pl.when(h < HG - 1)
@@ -270,6 +330,17 @@
         @pl.when(h < HG)
         def _():
             phase1(h, 1)
+
+        @pl.when(h < HG - 1)
+        def _():
+            forward(h + 1)
+
+        @pl.when(h > 0)
+        def _():
+            combine(h - 1)
+
+        @pl.when(h < HG)
+        def _():
             phase2(h, 0)
 
         @pl.when(h > 0)
@@ -284,47 +355,44 @@
         for r in others:
             for copy in arrive_g(h, r):
                 copy.wait_recv()
-            for copy in copies_a(h, r) + copies_b(h, r) + copies_g(h, r):
+            for copy in copies_a(h, r) + copies_g(h, r):
                 copy.wait_send()
-            copy_rq(h, r).wait_send()
-            copy_rkv(h, r).wait_send()
             copy_st(2 * h, r).wait_send()
             copy_st(2 * h + 1, r).wait_send()
+        for copy in copies_b(h) + copies_f(h) + copies_r1(h) + copies_r2(h):
+            copy.wait_send()
         return carry
 
     lax.fori_loop(0, HG, finish, 0)
 
-    for pair in range(SIDE * HG // 2):
-        cols = slice(pair * TOK, (pair + 1) * TOK)
+    image_rows = image_grad.shape[0]
+    for pair in range((heads + 1) // 2):
+        both = 2 * pair + 1 < heads
+        width = TOK if both else HEAD_DIM
+        cols = slice(pair * TOK, pair * TOK + width)
         first, second = f_kv[2 * pair].astype(F32), f_kv[2 * pair + 1].astype(F32)
-        query = jnp.concatenate([f_q[2 * pair], f_q[2 * pair + 1]], 0).astype(F32)
-        out_ref[0, :, cols] = query.T.astype(BF)
-        out_ref[1, :, cols] = jnp.concatenate([first[:, :HEAD_DIM], second[:, :HEAD_DIM]], 1).astype(BF)
-        out_ref[2, :, cols] = jnp.concatenate([first[:, HEAD_DIM:], second[:, HEAD_DIM:]], 1).astype(BF)
+        query = jnp.concatenate([f_q[2 * pair], f_q[2 * pair + 1]], 0).astype(F32).T
+        key = jnp.concatenate([first[:, :HEAD_DIM], second[:, :HEAD_DIM]], 1)
+        value = jnp.concatenate([first[:, HEAD_DIM:], second[:, HEAD_DIM:]], 1)
+        for i, whole in enumerate((query, key, value)):
+            image_out[i, :, cols] = whole[:image_rows, :width].astype(BF)
+            text_out[i, :, cols] = whole[image_rows:, :width].astype(BF)
 
 
 def body(image_qkv, text_qkv, image_grad, text_grad, text_len):
-    image_rows = image_qkv.shape[1]
-    width = image_qkv.shape[2]
-    heads = width // HEAD_DIM
     slots = SIDE * HG
-
-    def per_head(image, text):
-        whole = jnp.concatenate([image, text], 0).reshape(TOK, heads, HEAD_DIM)
-        return jnp.moveaxis(whole, 1, 0)
-
-    query, key, value = (per_head(image_qkv[i], text_qkv[i]) for i in range(3))
-    grad = per_head(image_grad, text_grad)
-    pad = ((0, slots - heads), (0, 0), (0, 0))
-    qg = jnp.pad(jnp.concatenate([query, grad], -1), pad)
-    kv = jnp.pad(jnp.concatenate([key, value], -1), pad)
     vmem = pl.BlockSpec(memory_space=pltpu.VMEM)
-    out = pl.pallas_call(
+    return pl.pallas_call(
         kernel,
-        out_shape=jax.ShapeDtypeStruct((3, TOK, slots * HEAD_DIM), BF),
-        in_specs=[pl.BlockSpec(memory_space=pltpu.SMEM), vmem, vmem],
-        out_specs=vmem,
+        out_shape=(
+            jax.ShapeDtypeStruct(image_qkv.shape, BF),
+            jax.ShapeDtypeStruct(text_qkv.shape, BF),
+        ),
+        in_specs=[pl.BlockSpec(memory_space=pltpu.SMEM), vmem, vmem, vmem, vmem],
+        out_specs=(vmem, vmem),
         scratch_shapes=[
+            pltpu.VMEM((slots, TOK, TOK), BF),
+            pltpu.VMEM((slots, TOK, TOK), BF),
             pltpu.VMEM((HG, SIDE, SIDE, TOK, TOK), BF),
             pltpu.VMEM((HG, SIDE, SIDE, TOK, TOK), BF),
             pltpu.VMEM((HG, SIDE, HEAD_DIM, ROWS), BF),
@@ -333,11 +401,13 @@
             pltpu.VMEM((2, 2, KEYS, ROWS), F32),
             pltpu.VMEM((KEYS, TOK), F32),
             pltpu.VMEM((KEYS, TOK), F32),
-            pltpu.VMEM((2 * HG, SIDE, 2, 8, ROWS), F32),
-            pltpu.VMEM((HG, SIDE, HEAD_DIM, ROWS), BF),
-            pltpu.VMEM((HG, SIDE, ROWS, TOK), BF),
-            pltpu.VMEM((HG, SIDE - 1, HEAD_DIM, ROWS), BF),
-            pltpu.VMEM((HG, SIDE - 1, ROWS, TOK), BF),
+            pltpu.VMEM((2 * HG, SIDE, 2, 16, TOK), F32),
+            pltpu.VMEM((HG, SIDE, 2, HEAD_DIM, ROWS // 2), BF),
+            pltpu.VMEM((HG, SIDE, 2, ROWS // 2, TOK), BF),
+            pltpu.VMEM((HG, 2, HEAD_DIM, ROWS // 2), BF),
+            pltpu.VMEM((HG, 2, ROWS // 2, TOK), BF),
+            pltpu.VMEM((HG, 2, 2, HEAD_DIM, ROWS // 2), BF),
+            pltpu.VMEM((HG, 2, 2, ROWS // 2, TOK), BF),
             pltpu.VMEM((HG, SIDE, HEAD_DIM, TOK), BF),
             pltpu.VMEM((HG, SIDE, TOK, TOK), BF),
             pltpu.VMEM((slots, HEAD_DIM, TOK), BF),
@@ -350,8 +420,7 @@
         compiler_params=pltpu.CompilerParams(
             collective_id=0, has_side_effects=True, vmem_limit_bytes=60 * 2**20
         ),
-    )(text_len, qg, kv)
-    return (out[:, :image_rows, :width], out[:, image_rows:, :width])
+    )(text_len, image_qkv, text_qkv, image_grad, text_grad)
 
 
 def solution(mesh):

time: 129 us -> 124 us (0.961)
  local copies, waits for them, and re-layouts: 7.89 us -> 2.81 us
  Pallas kernels: 116 us -> 120 us
  other arithmetic: 3.1 us -> 0 us
    slice x4 -> x0, local copies, waits for them, and re-layouts: 4.85 us -> none  [the longest x2 3.63 us: body(): return (out[:, :image_rows, :width], out[:, image_rows:, :width])]
    pallas_call x1, Pallas kernels: 116 us -> 120 us  [body(): pl.pallas_call(kernel, out_shape=(jax.ShapeDtypeStruct(image_qkv.shape, B...]
    concatenate x3 -> x0, other arithmetic: 2.58 us -> none  [the longest x1 1.21 us: body(): kv = jnp.pad(jnp.concatenate([key, value], -1), pad)]
    unnamed x11 -> x4, local copies, waits for them, and re-layouts: 1.46 us -> 2.81 us
where the time goes in v2:
time: 124 us
  Pallas kernels  120 us (97%)
  local copies, waits for them, and re-layouts  2.81 us (2%)
  between operations  1.29 us (1%)
    pallas_call x1, Pallas kernels, body(): pl.pallas_call(kernel, out_shape=(jax.ShapeDtypeStruct(image_qkv.shape, B...  120 us
    unnamed x4, local copies, waits for them, and re-layouts  2.81 us

profile of v2, /device:TPU:0, one launch (start us, length us, event | category | flops | bytes accessed | tf_op | source)
XLA Modules:
  0.0 124.3 jit_solution(16610023459763526519)
XLA Ops:
  1.3 120.2 %shard_map.68 = (bf16[3,120,1216]{2,1,0:T(8,128)(2,1)}, bf16[3,8,1216]{2,1,0:T(8,128)(2,1)}) custom-call(s32[1]{0:T(128)S(6)} %copy.9.tl_ref, bf16[3,120,1216]{2,1,0:T(8,128)(2,1)} %image_qkv.1, bf16[3,8,1216]{2,1,0:T(8,128)(2,1)} %text_qkv.1, bf16[120,1216]{1,0:T(8,128)(2,1)} %image_grad.1, bf16[8,1216]{1,0:T(8,128)(2,1)} %text_grad.1), custom_call_target="tpu_custom_call" | custom-call | tf_op jit(solution)/shard_map/pallas_call | solution.py:385
  121.5 0.0 copy-start
  121.5 2.2 %copy.10 = bf16[3,120,1216]{2,1,0:T(8,128)(2,1)} copy(bf16[3,120,1216]{2,1,0:T(8,128)(2,1)} %get-tuple-element.4) | data formatting | bytes 1751040
  123.6 0.0 copy-done
  123.7 0.6 copy.11
Async XLA Ops:
  121.5 2.2 %copy-start = (bf16[3,8,1216]{2,1,0:T(8,128)(2,1)S(1)}, bf16[3,8,1216]{2,1,0:T(8,128)(2,1)}, u32[]{:S(2)}) copy-start(bf16[3,8,1216]{2,1,0:T(8,128)(2,1)} %get-tuple-element.5) | copy-start | bytes 175108

commit v3 on v2

--- a/solution.py
+++ b/solution.py
@@ -28,7 +28,7 @@
 
 def kernel(
     tl_ref, image_qkv, text_qkv, image_grad, text_grad, image_out, text_out,
-    qg_own, kv_own, qg_all, kv_all, kt_all, s_ref, p_ref, dp_ref, ak, av, st,
+    qg_own, kv_own, qg_all, kv_all, kt_all, s_ref, p_ref, dp_ref, acc, st,
     dq_st, dkv_st, r1_q, r1_kv, r2_q, r2_kv, g_q, g_kv, f_q, f_kv,
     a_s, a_r, b_s, b_r, st_s, st_r, r_s, r_r, g_s, g_r,
 ):
@@ -73,42 +73,27 @@
             remote(kv_own.at[h], kv_all.at[h, z, f], a_s.at[1, h, r], a_r.at[1, h, r], at_x(f)),
         ]
 
-    def copies_b(h):
-        yn, yp, zn, zp = fwd(y, 1), back(y, 1), fwd(z, 1), back(z, 1)
-        return [
-            remote(qg_all.at[h, y], qg_all.at[h, y], b_s.at[0, h, 0], b_r.at[0, h, 0], at_y(yn)),
-            remote(kv_all.at[h, z], kv_all.at[h, z], b_s.at[1, h, 0], b_r.at[1, h, 0], at_z(zn)),
-            remote(qg_all.at[h, y], qg_all.at[h, y], b_s.at[0, h, 1], b_r.at[0, h, 1], at_y(yp)),
-            remote(kv_all.at[h, z], kv_all.at[h, z], b_s.at[1, h, 1], b_r.at[1, h, 1], at_z(zp)),
-        ]
-
-    def arrive_b(h):
-        yn, yp, zn, zp = fwd(y, 1), back(y, 1), fwd(z, 1), back(z, 1)
-        return [
-            remote(qg_all.at[h, yp], qg_all.at[h, yp], b_s.at[0, h, 0], b_r.at[0, h, 0], at_y(yp)),
-            remote(kv_all.at[h, zp], kv_all.at[h, zp], b_s.at[1, h, 0], b_r.at[1, h, 0], at_z(zp)),
-            remote(qg_all.at[h, yn], qg_all.at[h, yn], b_s.at[0, h, 1], b_r.at[0, h, 1], at_y(yn)),
-            remote(kv_all.at[h, zn], kv_all.at[h, zn], b_s.at[1, h, 1], b_r.at[1, h, 1], at_z(zn)),
-        ]
-
-    def relays(h, part, from_y, from_z, to_y, to_z):
-        half = pl.ds(part * 2, 2)
-        q = qg_all.at[h, from_y, half]
-        k = kv_all.at[h, from_z, half]
-        n = 2 + part
-        return [
-            remote(q, q, b_s.at[0, h, n], b_r.at[0, h, n], at_y(to_y)),
-            remote(k, k, b_s.at[1, h, n], b_r.at[1, h, n], at_z(to_z)),
-        ]
-
-    def copies_f(h):
-        yn, yp, zn, zp = fwd(y, 1), back(y, 1), fwd(z, 1), back(z, 1)
-        return relays(h, 0, yp, zp, yn, zn) + relays(h, 1, yn, zn, yp, zp)
-
-    def arrive_f(h):
-        yn, yp, zn, zp = fwd(y, 1), back(y, 1), fwd(z, 1), back(z, 1)
-        yo, zo = fwd(y, 2), fwd(z, 2)
-        return relays(h, 0, yo, zo, yp, zp) + relays(h, 1, yo, zo, yn, zn)
+    def move(arr, h, block, r, way, to, halves):
+        ref = (qg_all, kv_all)[arr].at[h, block, back(x, r)]
+        n = SIDE * (way + 2 * halves) + r
+        return remote(ref, ref, b_s.at[arr, h, n], b_r.at[arr, h, n], (at_y, at_z)[arr](to))
+
+    def copies_b(h, r):
+        return [move(a, h, i, r, w, (fwd, back)[w](i, 1), 0) for w in range(2) for a, i in enumerate((y, z))]
+
+    def arrive_b(h, r):
+        sides = [(a, w, (back, fwd)[w](i, 1)) for w in range(2) for a, i in enumerate((y, z))]
+        return [move(a, h, f, r, w, f, 0) for a, w, f in sides]
+
+    def copies_f(h, r):
+        w = r % 2
+        sides = [(a, (back, fwd)[w](i, 1), (fwd, back)[w](i, 1)) for a, i in enumerate((y, z))]
+        return [move(a, h, f, r, w, t, 1) for a, f, t in sides]
+
+    def arrive_f(h, r):
+        w = r % 2
+        sides = [(a, fwd(i, 2), (back, fwd)[w](i, 1)) for a, i in enumerate((y, z))]
+        return [move(a, h, f, r, w, t, 1) for a, f, t in sides]
 
     def copy_st(u, r):
         return remote(st.at[u, 0], st.at[u, r], st_s.at[u, r], st_r.at[u, r], at_y(fwd(y, r)))
@@ -174,105 +159,108 @@
         qg_all[h, y, x] = qg_own[HG * x + h]
         kv_all[h, z, x] = kv_own[HG * x + h]
 
+    order = (0, 1, 3, 2)
+
     def spread(h):
-        for r in others:
-            for copy in arrive_a(h, r):
+        for r in order:
+            if r:
+                for copy in arrive_a(h, r):
+                    copy.wait_recv()
+            for copy in copies_b(h, r):
+                copy.start()
+
+    def forward(h):
+        for r in order:
+            for copy in arrive_b(h, r):
                 copy.wait_recv()
-        for copy in copies_b(h):
-            copy.start()
-
-    def forward(h):
-        for copy in arrive_b(h):
-            copy.wait_recv()
-        for copy in copies_f(h):
-            copy.start()
+            for copy in copies_f(h, r):
+                copy.start()
 
     def receive(h):
-        for copy in arrive_f(h):
-            copy.wait_recv()
+        for r in order:
+            for copy in arrive_f(h, r):
+                copy.wait_recv()
         for k in range(SIDE):
             kt_all[h, k] = kv_all[h, k].reshape(ROWS, TOK).T[:HEAD_DIM]
 
     def phase1(h, half):
-        def block(j, carry):
+        count = 2 * ROWS
+        qg = qg_all[h, 2 * half : 2 * half + 2].reshape(count, TOK)
+        lane = lax.broadcasted_iota(jnp.int32, qg.shape, 1)
+        q0 = jnp.where(lane < HEAD_DIM, qg, jnp.zeros_like(qg))
+        g0 = jnp.where(lane < HEAD_DIM, jnp.zeros_like(qg), qg)
+        sub = lax.broadcasted_iota(jnp.int32, (8, count), 0)
+        top = jnp.full((8, count), NEG, F32)
+        for k in range(SIDE):
+            s = dot(kv_all[h, k].reshape(ROWS, TOK), q0, NT)
+            s_ref[k * ROWS : (k + 1) * ROWS, :] = s
+            parts = s.reshape(SIDE, TOK // 8, 8, count)
+            top = jnp.maximum(top, jnp.max(parts[:, : TOK // 8 - 1].reshape(-1, 8, count), axis=0))
+            for i in range(SIDE):
+                valid = (y * 16 + k * 4 + i) * 8 + sub < tl_ref[0]
+                text = jnp.where(valid, parts[i, TOK // 8 - 1], NEG)
+                end = k * ROWS + (i + 1) * TOK
+                s_ref[end - 8 : end, :] = text
+                top = jnp.maximum(top, text)
+        top = jnp.max(top, axis=0, keepdims=True) * LOG
+        total = jnp.zeros((8, count), F32)
+        weighted = jnp.zeros((8, count), F32)
+        for k in range(SIDE):
+            rows = slice(k * ROWS, (k + 1) * ROWS)
+            d = dot(kv_all[h, k].reshape(ROWS, TOK), g0, NT)
+            p = jnp.exp2(s_ref[rows, :] * LOG - top)
+            total += jnp.sum(p.reshape(-1, 8, count), axis=0)
+            weighted += jnp.sum((p * d).reshape(-1, 8, count), axis=0)
+            p_ref[half, rows, :] = p.astype(BF)
+            dp_ref[half, rows, :] = d
+        stats = (top, jnp.sum(total, axis=0, keepdims=True), jnp.sum(weighted, axis=0, keepdims=True))
+        parts = [s[:, i * TOK : (i + 1) * TOK] for s in stats for i in range(2 * SIDE)]
+        st[2 * h + half, 0] = jnp.concatenate(parts, 0)
+        for r in others:
+            copy_st(2 * h + half, r).start()
+
+    def phase2(h, half):
+        u = 2 * h + half
+        for r in others:
+            copy_st(u, r).wait_recv()
+        stats = [st[u, r] for r in range(SIDE)]
+        tops = [s[0:8] for s in stats]
+        top = jnp.maximum(jnp.maximum(tops[0], tops[1]), jnp.maximum(tops[2], tops[3]))
+        parts = [jnp.exp2(t - top) for t in tops]
+        total = sum(s[8:16] * e for s, e in zip(stats, parts))
+        factors = parts[0] / total
+        deltas = sum(s[16:24] * e for s, e in zip(stats, parts)) / total
+        for j in range(2):
+            factor, delta = (
+                jnp.concatenate([v[i : i + 1] for i in range(SIDE * j, SIDE * (j + 1))], 1)
+                for v in (factors, deltas)
+            )
             qg = qg_all[h, 2 * half + j].reshape(ROWS, TOK)
             lane = lax.broadcasted_iota(jnp.int32, qg.shape, 1)
             q0 = jnp.where(lane < HEAD_DIM, qg, jnp.zeros_like(qg))
             g0 = jnp.where(lane < HEAD_DIM, jnp.zeros_like(qg), qg)
-            sub = lax.broadcasted_iota(jnp.int32, (8, ROWS), 0)
-            top = jnp.full((8, ROWS), NEG, F32)
-            for k in range(SIDE):
-                s = dot(kv_all[h, k].reshape(ROWS, TOK), q0, NT)
-                s_ref[k * ROWS : (k + 1) * ROWS, :] = s
-                parts = s.reshape(SIDE, TOK // 8, 8, ROWS)
-                top = jnp.maximum(top, jnp.max(parts[:, : TOK // 8 - 1].reshape(-1, 8, ROWS), axis=0))
-                for i in range(SIDE):
-                    valid = (y * 16 + k * 4 + i) * 8 + sub < tl_ref[0]
-                    text = jnp.where(valid, parts[i, TOK // 8 - 1], NEG)
-                    end = k * ROWS + (i + 1) * TOK
-                    s_ref[end - 8 : end, :] = text
-                    top = jnp.maximum(top, text)
-            top = jnp.max(top, axis=0, keepdims=True) * LOG
-            total = jnp.zeros((8, ROWS), F32)
-            weighted = jnp.zeros((8, ROWS), F32)
-            for k in range(SIDE):
-                rows = slice(k * ROWS, (k + 1) * ROWS)
-                d = dot(kv_all[h, k].reshape(ROWS, TOK), g0, NT)
-                p = jnp.exp2(s_ref[rows, :] * LOG - top)
-                total += jnp.sum(p.reshape(-1, 8, ROWS), axis=0)
-                weighted += jnp.sum((p * d).reshape(-1, 8, ROWS), axis=0)
-                p_ref[half, j, rows, :] = p.astype(BF)
-                dp_ref[half, j, rows, :] = d
-            stats = (top, jnp.sum(total, axis=0, keepdims=True), jnp.sum(weighted, axis=0, keepdims=True))
-            parts = [s[:, i * TOK : (i + 1) * TOK] for s in stats for i in range(SIDE)]
-            st[2 * h + half, 0, j] = jnp.concatenate(parts + [jnp.zeros((SIDE, TOK), F32)], 0)
-            return carry
-
-        lax.fori_loop(0, 2, block, 0)
-        for r in others:
-            copy_st(2 * h + half, r).start()
-
-    def phase2(h, half):
-        u = 2 * h + half
-        for r in others:
-            copy_st(u, r).wait_recv()
-        if half == 0:
-            ak[...] = jnp.zeros_like(ak)
-            av[...] = jnp.zeros_like(av)
-
-        def block(j, carry):
-            stats = [st[u, r, j] for r in range(SIDE)]
-            tops = [s[0:4] for s in stats]
-            top = jnp.maximum(jnp.maximum(tops[0], tops[1]), jnp.maximum(tops[2], tops[3]))
-            parts = [jnp.exp2(t - top) for t in tops]
-            total = sum(s[4:8] * e for s, e in zip(stats, parts))
-            factor = parts[0] / total
-            delta = sum(s[8:12] * e for s, e in zip(stats, parts)) / total
-            factor, delta = (
-                jnp.concatenate([v[i : i + 1] for i in range(SIDE)], 1) for v in (factor, delta)
-            )
-            qg = qg_all[h, 2 * half + j].reshape(ROWS, TOK)
+            cols = slice(j * ROWS, (j + 1) * ROWS)
             dq = jnp.zeros((HEAD_DIM, ROWS), F32)
             for c in range(KEYS // CHUNK):
                 rows = slice(c * CHUNK, (c + 1) * CHUNK)
-                p = p_ref[half, j, rows, :].astype(F32) * factor
-                ds = (p * (dp_ref[half, j, rows, :] - delta)).astype(BF)
-                av[rows, :] += dot(p.astype(BF), qg, NN)
-                ak[rows, :] += dot(ds, qg, NN)
+                p = p_ref[half, rows, cols].astype(F32) * factor
+                ds = (p * (dp_ref[half, rows, cols] - delta)).astype(BF)
+                part = dot(p.astype(BF), g0, NN) + dot(ds, q0, NN)
+                if half == 0 and j == 0:
+                    acc[rows, :] = part
+                else:
+                    acc[rows, :] += part
                 per = ROWS // CHUNK
-                part = c % per * CHUNK
-                dq += dot(kt_all[h, c // per, :, part : part + CHUNK], ds, NN)
+                at = c % per * CHUNK
+                dq += dot(kt_all[h, c // per, :, at : at + CHUNK], ds, NN)
             dq = (dq * SCALE).astype(BF)
             for i in range(2):
                 dq_st[h, 2 * half + j, i] = dq[:, i * ROWS // 2 : (i + 1) * ROWS // 2]
-            return carry
-
-        lax.fori_loop(0, 2, block, 0)
         if half == 1:
             lane = lax.broadcasted_iota(jnp.int32, (ROWS, TOK), 1)
             for k in range(SIDE):
                 rows = slice(k * ROWS, (k + 1) * ROWS)
-                dkv = jnp.where(lane < HEAD_DIM, ak[rows, :] * SCALE, av[rows, :]).astype(BF)
+                dkv = (acc[rows, :] * jnp.where(lane < HEAD_DIM, SCALE, 1.0)).astype(BF)
                 dkv_st[h, k] = dkv.reshape(2, ROWS // 2, TOK)
             for copy in copies_r1(h):
                 copy.start()
@@ -323,6 +311,10 @@
         def _():
             spread(h + 1)
 
+        @pl.when((h > 1) & (h < HG))
+        def _():
+            hand_over(h - 2)
+
         @pl.when(h > 0)
         def _():
             phase2(h - 1, 1)
@@ -335,6 +327,10 @@
         def _():
             forward(h + 1)
 
+        @pl.when(h == HG)
+        def _():
+            hand_over(HG - 2)
+
         @pl.when(h > 0)
         def _():
             combine(h - 1)
@@ -343,9 +339,9 @@
         def _():
             phase2(h, 0)
 
-        @pl.when(h > 0)
-        def _():
-            hand_over(h - 1)
+        @pl.when(h == HG)
+        def _():
+            hand_over(HG - 1)
 
         return carry
 
@@ -355,11 +351,11 @@
         for r in others:
             for copy in arrive_g(h, r):
                 copy.wait_recv()
-            for copy in copies_a(h, r) + copies_g(h, r):
+            for copy in copies_a(h, r) + copies_g(h, r) + copies_b(h, r) + copies_f(h, r):
                 copy.wait_send()
             copy_st(2 * h, r).wait_send()
             copy_st(2 * h + 1, r).wait_send()
-        for copy in copies_b(h) + copies_f(h) + copies_r1(h) + copies_r2(h):
+        for copy in copies_b(h, 0) + copies_f(h, 0) + copies_r1(h) + copies_r2(h):
             copy.wait_send()
         return carry
 
@@ -396,12 +392,11 @@
             pltpu.VMEM((HG, SIDE, SIDE, TOK, TOK), BF),
             pltpu.VMEM((HG, SIDE, SIDE, TOK, TOK), BF),
             pltpu.VMEM((HG, SIDE, HEAD_DIM, ROWS), BF),
-            pltpu.VMEM((KEYS, ROWS), F32),
-            pltpu.VMEM((2, 2, KEYS, ROWS), BF),
-            pltpu.VMEM((2, 2, KEYS, ROWS), F32),
+            pltpu.VMEM((KEYS, 2 * ROWS), F32),
+            pltpu.VMEM((2, KEYS, 2 * ROWS), BF),
+            pltpu.VMEM((2, KEYS, 2 * ROWS), F32),
             pltpu.VMEM((KEYS, TOK), F32),
-            pltpu.VMEM((KEYS, TOK), F32),
-            pltpu.VMEM((2 * HG, SIDE, 2, 16, TOK), F32),
+            pltpu.VMEM((2 * HG, SIDE, 6 * SIDE, TOK), F32),
             pltpu.VMEM((HG, SIDE, 2, HEAD_DIM, ROWS // 2), BF),
             pltpu.VMEM((HG, SIDE, 2, ROWS // 2, TOK), BF),
             pltpu.VMEM((HG, 2, HEAD_DIM, ROWS // 2), BF),
@@ -415,7 +410,10 @@
         ]
         + [
             pltpu.SemaphoreType.DMA(shape)
-            for shape in [(2, HG, SIDE)] * 4 + [(2 * HG, SIDE)] * 2 + [(2, HG, SIDE)] * 4
+            for shape in [(2, HG, SIDE)] * 2
+            + [(2, HG, SIDE * SIDE)] * 2
+            + [(2 * HG, SIDE)] * 2
+            + [(2, HG, SIDE)] * 4
         ],
         compiler_params=pltpu.CompilerParams(
             collective_id=0, has_side_effects=True, vmem_limit_bytes=60 * 2**20

time: 124 us -> 116 us (0.935)
  Pallas kernels: 120 us -> 112 us
    pallas_call x1, Pallas kernels: 120 us -> 112 us  [body(): pl.pallas_call(kernel, out_shape=(jax.ShapeDtypeStruct(image_qkv.shape, B...]
where the time goes in v3:
time: 116 us
  Pallas kernels  112 us (97%)
  local copies, waits for them, and re-layouts  2.81 us (2%)
  between operations  1.29 us (1%)
    pallas_call x1, Pallas kernels, body(): pl.pallas_call(kernel, out_shape=(jax.ShapeDtypeStruct(image_qkv.shape, B...  112 us
    unnamed x4, local copies, waits for them, and re-layouts  2.81 us

profile of v3, /device:TPU:0, one launch (start us, length us, event | category | flops | bytes accessed | tf_op | source)
XLA Modules:
  0.0 116.0 jit_solution(9368872201280482190)
XLA Ops:
  1.3 111.9 %shard_map.68 = (bf16[3,120,1216]{2,1,0:T(8,128)(2,1)}, bf16[3,8,1216]{2,1,0:T(8,128)(2,1)}) custom-call(s32[1]{0:T(128)S(6)} %copy.9.tl_ref, bf16[3,120,1216]{2,1,0:T(8,128)(2,1)} %image_qkv.1, bf16[3,8,1216]{2,1,0:T(8,128)(2,1)} %text_qkv.1, bf16[120,1216]{1,0:T(8,128)(2,1)} %image_grad.1, bf16[8,1216]{1,0:T(8,128)(2,1)} %text_grad.1), custom_call_target="tpu_custom_call" | custom-call | tf_op jit(solution)/shard_map/pallas_call | solution.py:381
  113.2 0.0 copy-start
  113.2 2.2 %copy.10 = bf16[3,120,1216]{2,1,0:T(8,128)(2,1)} copy(bf16[3,120,1216]{2,1,0:T(8,128)(2,1)} %get-tuple-element.4) | data formatting | bytes 1751040
  115.4 0.0 copy-done
  115.4 0.6 copy.11
Async XLA Ops:
  113.2 2.2 %copy-start = (bf16[3,8,1216]{2,1,0:T(8,128)(2,1)S(1)}, bf16[3,8,1216]{2,1,0:T(8,128)(2,1)}, u32[]{:S(2)}) copy-start(bf16[3,8,1216]{2,1,0:T(8,128)(2,1)} %get-tuple-element.5) | copy-start | bytes 175108

commit v4 on v3

--- a/solution.py
+++ b/solution.py
@@ -30,7 +30,7 @@
     tl_ref, image_qkv, text_qkv, image_grad, text_grad, image_out, text_out,
     qg_own, kv_own, qg_all, kv_all, kt_all, s_ref, p_ref, dp_ref, acc, st,
     dq_st, dkv_st, r1_q, r1_kv, r2_q, r2_kv, g_q, g_kv, f_q, f_kv,
-    a_s, a_r, b_s, b_r, st_s, st_r, r_s, r_r, g_s, g_r,
+    sent, a_r, b_r, f_r, st_r, r_r, g_r,
 ):
     seq = lax.axis_index("seq")
     core = lax.axis_index("head")
@@ -62,71 +62,59 @@
     def copies_a(h, r):
         t = fwd(x, r)
         return [
-            remote(qg_own.at[HG * t + h], qg_all.at[h, y, x], a_s.at[0, h, r], a_r.at[0, h, r], at_x(t)),
-            remote(kv_own.at[HG * t + h], kv_all.at[h, z, x], a_s.at[1, h, r], a_r.at[1, h, r], at_x(t)),
+            remote(qg_own.at[HG * t + h], qg_all.at[h, y, x], sent.at[0], a_r.at[h, r - 1], at_x(t)),
+            remote(kv_own.at[HG * t + h], kv_all.at[h, z, x], sent.at[0], a_r.at[h, r - 1], at_x(t)),
         ]
 
-    def arrive_a(h, r):
+    def arrived(ref, sem):
+        remote(ref, ref, sem, sem, (seq, core)).wait_recv()
+
+    def gone(ref, sem):
+        remote(ref, ref, sem, sem, (seq, core)).wait_send()
+
+    def copies_b(h, r):
         f = back(x, r)
+        q, k = qg_all.at[h, y, f], kv_all.at[h, z, f]
+        sems = (sent.at[1], b_r.at[h, r])
         return [
-            remote(qg_own.at[h], qg_all.at[h, y, f], a_s.at[0, h, r], a_r.at[0, h, r], at_x(f)),
-            remote(kv_own.at[h], kv_all.at[h, z, f], a_s.at[1, h, r], a_r.at[1, h, r], at_x(f)),
+            remote(q, q, *sems, at_y(fwd(y, 1))),
+            remote(k, k, *sems, at_z(fwd(z, 1))),
+            remote(q, q, *sems, at_y(back(y, 1))),
+            remote(k, k, *sems, at_z(back(z, 1))),
         ]
 
-    def move(arr, h, block, r, way, to, halves):
-        ref = (qg_all, kv_all)[arr].at[h, block, back(x, r)]
-        n = SIDE * (way + 2 * halves) + r
-        return remote(ref, ref, b_s.at[arr, h, n], b_r.at[arr, h, n], (at_y, at_z)[arr](to))
-
-    def copies_b(h, r):
-        return [move(a, h, i, r, w, (fwd, back)[w](i, 1), 0) for w in range(2) for a, i in enumerate((y, z))]
-
-    def arrive_b(h, r):
-        sides = [(a, w, (back, fwd)[w](i, 1)) for w in range(2) for a, i in enumerate((y, z))]
-        return [move(a, h, f, r, w, f, 0) for a, w, f in sides]
-
     def copies_f(h, r):
-        w = r % 2
-        sides = [(a, (back, fwd)[w](i, 1), (fwd, back)[w](i, 1)) for a, i in enumerate((y, z))]
-        return [move(a, h, f, r, w, t, 1) for a, f, t in sides]
-
-    def arrive_f(h, r):
-        w = r % 2
-        sides = [(a, fwd(i, 2), (back, fwd)[w](i, 1)) for a, i in enumerate((y, z))]
-        return [move(a, h, f, r, w, t, 1) for a, f, t in sides]
+        come, go = (back, fwd) if r % 2 == 0 else (fwd, back)
+        f = back(x, r)
+        q, k = qg_all.at[h, come(y, 1), f], kv_all.at[h, come(z, 1), f]
+        sems = (sent.at[2], f_r.at[h])
+        return [remote(q, q, *sems, at_y(go(y, 1))), remote(k, k, *sems, at_z(go(z, 1)))]
 
     def copy_st(u, r):
-        return remote(st.at[u, 0], st.at[u, r], st_s.at[u, r], st_r.at[u, r], at_y(fwd(y, r)))
+        return remote(st.at[u, 0], st.at[u, r], sent.at[3], st_r.at[u], at_y(fwd(y, r)))
 
     def copies_r1(h):
         yo, zo = fwd(y, 2), fwd(z, 2)
         places = ((at_y(fwd(y, 1)), at_z(fwd(z, 1))), (at_y(back(y, 1)), at_z(back(z, 1))))
         copies = []
         for n, (to_y, to_z) in enumerate(places):
-            copies.append(remote(dq_st.at[h, yo, n], r1_q.at[h, n], r_s.at[0, h, n], r_r.at[0, h, n], to_y))
-            copies.append(remote(dkv_st.at[h, zo, n], r1_kv.at[h, n], r_s.at[1, h, n], r_r.at[1, h, n], to_z))
+            copies.append(remote(dq_st.at[h, yo, n], r1_q.at[h, n], sent.at[4], r_r.at[0, h], to_y))
+            copies.append(remote(dkv_st.at[h, zo, n], r1_kv.at[h, n], sent.at[5], r_r.at[1, h], to_z))
         return copies
 
     def copies_r2(h):
         copies = []
         for n, (ty, tz) in enumerate(((fwd(y, 1), fwd(z, 1)), (back(y, 1), back(z, 1)))):
             k = 2 + n
-            copies.append(remote(dq_st.at[h, ty], r2_q.at[h, n], r_s.at[0, h, k], r_r.at[0, h, k], at_y(ty)))
-            copies.append(remote(dkv_st.at[h, tz], r2_kv.at[h, n], r_s.at[1, h, k], r_r.at[1, h, k], at_z(tz)))
+            copies.append(remote(dq_st.at[h, ty], r2_q.at[h, n], sent.at[6], r_r.at[2, h], at_y(ty)))
+            copies.append(remote(dkv_st.at[h, tz], r2_kv.at[h, n], sent.at[7], r_r.at[3, h], at_z(tz)))
         return copies
 
     def copies_g(h, r):
         t = fwd(x, r)
         return [
-            remote(g_q.at[h, t], f_q.at[HG * x + h], g_s.at[0, h, r], g_r.at[0, h, r], at_x(t)),
-            remote(g_kv.at[h, t], f_kv.at[HG * x + h], g_s.at[1, h, r], g_r.at[1, h, r], at_x(t)),
-        ]
-
-    def arrive_g(h, r):
-        f = back(x, r)
-        return [
-            remote(g_q.at[h, f], f_q.at[HG * f + h], g_s.at[0, h, r], g_r.at[0, h, r], at_x(f)),
-            remote(g_kv.at[h, f], f_kv.at[HG * f + h], g_s.at[1, h, r], g_r.at[1, h, r], at_x(f)),
+            remote(g_q.at[h, t], f_q.at[HG * x + h], sent.at[8], g_r.at[0, h], at_x(t)),
+            remote(g_kv.at[h, t], f_kv.at[HG * x + h], sent.at[9], g_r.at[1, h], at_x(t)),
         ]
 
     barrier = pltpu.get_barrier_semaphore()
@@ -164,22 +152,18 @@
     def spread(h):
         for r in order:
             if r:
-                for copy in arrive_a(h, r):
-                    copy.wait_recv()
+                arrived(qg_all.at[h, 0, pl.ds(0, 2)], a_r.at[h, r - 1])
             for copy in copies_b(h, r):
                 copy.start()
 
     def forward(h):
         for r in order:
-            for copy in arrive_b(h, r):
-                copy.wait_recv()
+            arrived(qg_all.at[h, 0], b_r.at[h, r])
             for copy in copies_f(h, r):
                 copy.start()
 
     def receive(h):
-        for r in order:
-            for copy in arrive_f(h, r):
-                copy.wait_recv()
+        arrived(qg_all.at[h, pl.ds(0, 2)], f_r.at[h])
         for k in range(SIDE):
             kt_all[h, k] = kv_all[h, k].reshape(ROWS, TOK).T[:HEAD_DIM]
 
@@ -221,8 +205,7 @@
 
     def phase2(h, half):
         u = 2 * h + half
-        for r in others:
-            copy_st(u, r).wait_recv()
+        arrived(st.at[u, pl.ds(1, SIDE - 1)], st_r.at[u])
         stats = [st[u, r] for r in range(SIDE)]
         tops = [s[0:8] for s in stats]
         top = jnp.maximum(jnp.maximum(tops[0], tops[1]), jnp.maximum(tops[2], tops[3]))
@@ -266,8 +249,8 @@
                 copy.start()
 
     def combine(h):
-        for copy in copies_r1(h):
-            copy.wait_recv()
+        arrived(r1_q.at[h], r_r.at[0, h])
+        arrived(r1_kv.at[h], r_r.at[1, h])
         for n, (ty, tz) in enumerate(((fwd(y, 1), fwd(z, 1)), (back(y, 1), back(z, 1)))):
             dq_st[h, ty, n] = (dq_st[h, ty, n].astype(F32) + r1_q[h, n].astype(F32)).astype(BF)
             dkv_st[h, tz, n] = (dkv_st[h, tz, n].astype(F32) + r1_kv[h, n].astype(F32)).astype(BF)
@@ -275,8 +258,8 @@
             copy.start()
 
     def hand_over(h):
-        for copy in copies_r2(h):
-            copy.wait_recv()
+        arrived(r2_q.at[h], r_r.at[2, h])
+        arrived(r2_kv.at[h], r_r.at[3, h])
         for i in range(2):
             dq = dq_st[h, y, i].astype(F32) + r2_q[h, 0, i].astype(F32) + r2_q[h, 1, i].astype(F32)
             dkv = dkv_st[h, z, i].astype(F32) + r2_kv[h, 0, i].astype(F32) + r2_kv[h, 1, i].astype(F32)
@@ -348,18 +331,25 @@
     lax.fori_loop(0, HG + 1, step, 0)
 
     def finish(h, carry):
-        for r in others:
-            for copy in arrive_g(h, r):
-                copy.wait_recv()
-            for copy in copies_a(h, r) + copies_g(h, r) + copies_b(h, r) + copies_f(h, r):
-                copy.wait_send()
-            copy_st(2 * h, r).wait_send()
-            copy_st(2 * h + 1, r).wait_send()
-        for copy in copies_b(h, 0) + copies_f(h, 0) + copies_r1(h) + copies_r2(h):
-            copy.wait_send()
+        arrived(g_q.at[h, pl.ds(0, SIDE - 1)], g_r.at[0, h])
+        arrived(g_kv.at[h, pl.ds(0, SIDE - 1)], g_r.at[1, h])
         return carry
 
     lax.fori_loop(0, HG, finish, 0)
+    moved = (
+        qg_all.at[:, pl.ds(0, 2), pl.ds(0, SIDE - 1)],
+        qg_all,
+        qg_all.at[:, pl.ds(0, 2)],
+        st.at[:, pl.ds(0, SIDE - 1)],
+        r1_q,
+        r1_kv,
+        r2_q,
+        r2_kv,
+        g_q.at[:, pl.ds(0, SIDE - 1)],
+        g_kv.at[:, pl.ds(0, SIDE - 1)],
+    )
+    for i, ref in enumerate(moved):
+        gone(ref, sent.at[i])
 
     image_rows = image_grad.shape[0]
     for pair in range((heads + 1) // 2):
@@ -410,10 +400,7 @@
         ]
         + [
             pltpu.SemaphoreType.DMA(shape)
-            for shape in [(2, HG, SIDE)] * 2
-            + [(2, HG, SIDE * SIDE)] * 2
-            + [(2 * HG, SIDE)] * 2
-            + [(2, HG, SIDE)] * 4
+            for shape in [(10,), (HG, SIDE - 1), (HG, SIDE), (HG,), (2 * HG,), (4, HG), (2, HG)]
         ],
         compiler_params=pltpu.CompilerParams(
             collective_id=0, has_side_effects=True, vmem_limit_bytes=60 * 2**20

time: 116 us -> 111 us (0.957)
  Pallas kernels: 112 us -> 107 us
    pallas_call x1, Pallas kernels: 112 us -> 107 us  [body(): pl.pallas_call(kernel, out_shape=(jax.ShapeDtypeStruct(image_qkv.shape, B...]
where the time goes in v4:
time: 111 us
  Pallas kernels  107 us (96%)
  local copies, waits for them, and re-layouts  2.81 us (3%)
  between operations  1.29 us (1%)
    pallas_call x1, Pallas kernels, body(): pl.pallas_call(kernel, out_shape=(jax.ShapeDtypeStruct(image_qkv.shape, B...  107 us
    unnamed x4, local copies, waits for them, and re-layouts  2.81 us

profile of v4, /device:TPU:0, one launch (start us, length us, event | category | flops | bytes accessed | tf_op | source)
XLA Modules:
  0.0 110.9 jit_solution(15186638739598172640)
XLA Ops:
  1.3 106.8 %shard_map.68 = (bf16[3,120,1216]{2,1,0:T(8,128)(2,1)}, bf16[3,8,1216]{2,1,0:T(8,128)(2,1)}) custom-call(s32[1]{0:T(128)S(6)} %copy.9.tl_ref, bf16[3,120,1216]{2,1,0:T(8,128)(2,1)} %image_qkv.1, bf16[3,8,1216]{2,1,0:T(8,128)(2,1)} %text_qkv.1, bf16[120,1216]{1,0:T(8,128)(2,1)} %image_grad.1, bf16[8,1216]{1,0:T(8,128)(2,1)} %text_grad.1), custom_call_target="tpu_custom_call" | custom-call | tf_op jit(solution)/shard_map/pallas_call | solution.py:371
  108.1 0.0 copy-start
  108.1 2.2 %copy.10 = bf16[3,120,1216]{2,1,0:T(8,128)(2,1)} copy(bf16[3,120,1216]{2,1,0:T(8,128)(2,1)} %get-tuple-element.4) | data formatting | bytes 1751040
  110.3 0.0 copy-done
  110.3 0.6 copy.11
Async XLA Ops:
  108.1 2.2 %copy-start = (bf16[3,8,1216]{2,1,0:T(8,128)(2,1)S(1)}, bf16[3,8,1216]{2,1,0:T(8,128)(2,1)}, u32[]{:S(2)}) copy-start(bf16[3,8,1216]{2,1,0:T(8,128)(2,1)} %get-tuple-element.5) | copy-start | bytes 175108

commit v5 on v4

--- a/solution.py
+++ b/solution.py
@@ -93,29 +93,29 @@
     def copy_st(u, r):
         return remote(st.at[u, 0], st.at[u, r], sent.at[3], st_r.at[u], at_y(fwd(y, r)))
 
-    def copies_r1(h):
-        yo, zo = fwd(y, 2), fwd(z, 2)
-        places = ((at_y(fwd(y, 1)), at_z(fwd(z, 1))), (at_y(back(y, 1)), at_z(back(z, 1))))
-        copies = []
-        for n, (to_y, to_z) in enumerate(places):
-            copies.append(remote(dq_st.at[h, yo, n], r1_q.at[h, n], sent.at[4], r_r.at[0, h], to_y))
-            copies.append(remote(dkv_st.at[h, zo, n], r1_kv.at[h, n], sent.at[5], r_r.at[1, h], to_z))
-        return copies
-
-    def copies_r2(h):
-        copies = []
-        for n, (ty, tz) in enumerate(((fwd(y, 1), fwd(z, 1)), (back(y, 1), back(z, 1)))):
-            k = 2 + n
-            copies.append(remote(dq_st.at[h, ty], r2_q.at[h, n], sent.at[6], r_r.at[2, h], at_y(ty)))
-            copies.append(remote(dkv_st.at[h, tz], r2_kv.at[h, n], sent.at[7], r_r.at[3, h], at_z(tz)))
-        return copies
-
-    def copies_g(h, r):
+    def copies_r1(h, kv):
+        src, dst, at, i = (dkv_st, r1_kv, at_z, z) if kv else (dq_st, r1_q, at_y, y)
+        return [
+            remote(src.at[h, fwd(i, 2), n], dst.at[h, n], sent.at[4 + kv], r_r.at[kv, h], at(t))
+            for n, t in enumerate((fwd(i, 1), back(i, 1)))
+        ]
+
+    def copies_r2(h, kv):
+        if not kv:
+            return [
+                remote(dq_st.at[h, t], r2_q.at[h, n], sent.at[6], r_r.at[2, h], at_y(t))
+                for n, t in enumerate((fwd(y, 1), back(y, 1)))
+            ]
+        return [
+            remote(dkv_st.at[h, t, i], r2_kv.at[h, n, i], sent.at[7], r_r.at[3 + i, h], at_z(t))
+            for i in range(2)
+            for n, t in enumerate((fwd(z, 1), back(z, 1)))
+        ]
+
+    def copy_g(h, r, kv):
+        src, dst = (g_kv, f_kv) if kv else (g_q, f_q)
         t = fwd(x, r)
-        return [
-            remote(g_q.at[h, t], f_q.at[HG * x + h], sent.at[8], g_r.at[0, h], at_x(t)),
-            remote(g_kv.at[h, t], f_kv.at[HG * x + h], sent.at[9], g_r.at[1, h], at_x(t)),
-        ]
+        return remote(src.at[h, t], dst.at[HG * x + h], sent.at[8 + kv], g_r.at[kv, h], at_x(t))
 
     barrier = pltpu.get_barrier_semaphore()
     for r in others:
@@ -203,8 +203,7 @@
         for r in others:
             copy_st(2 * h + half, r).start()
 
-    def phase2(h, half):
-        u = 2 * h + half
+    def row_terms(u):
         arrived(st.at[u, pl.ds(1, SIDE - 1)], st_r.at[u])
         stats = [st[u, r] for r in range(SIDE)]
         tops = [s[0:8] for s in stats]
@@ -213,15 +212,31 @@
         total = sum(s[8:16] * e for s, e in zip(stats, parts))
         factors = parts[0] / total
         deltas = sum(s[16:24] * e for s, e in zip(stats, parts)) / total
+        return [
+            [jnp.concatenate([v[i : i + 1] for i in range(SIDE * j, SIDE * (j + 1))], 1) for v in (factors, deltas)]
+            for j in range(2)
+        ]
+
+    def apart(qg):
+        lane = lax.broadcasted_iota(jnp.int32, qg.shape, 1)
+        zero = jnp.zeros_like(qg)
+        return jnp.where(lane < HEAD_DIM, qg, zero), jnp.where(lane < HEAD_DIM, zero, qg)
+
+    def keep_dq(h, slot, dq):
+        dq = (dq * SCALE).astype(BF)
+        for i in range(2):
+            dq_st[h, slot, i] = dq[:, i * ROWS // 2 : (i + 1) * ROWS // 2]
+
+    def keep_dkv(h, k, dkv):
+        lane = lax.broadcasted_iota(jnp.int32, dkv.shape, 1)
+        dkv = (dkv * jnp.where(lane < HEAD_DIM, SCALE, 1.0)).astype(BF)
+        dkv_st[h, k] = dkv.reshape(2, ROWS // 2, TOK)
+
+    def phase2(h, half):
+        terms = row_terms(2 * h + half)
         for j in range(2):
-            factor, delta = (
-                jnp.concatenate([v[i : i + 1] for i in range(SIDE * j, SIDE * (j + 1))], 1)
-                for v in (factors, deltas)
-            )
-            qg = qg_all[h, 2 * half + j].reshape(ROWS, TOK)
-            lane = lax.broadcasted_iota(jnp.int32, qg.shape, 1)
-            q0 = jnp.where(lane < HEAD_DIM, qg, jnp.zeros_like(qg))
-            g0 = jnp.where(lane < HEAD_DIM, jnp.zeros_like(qg), qg)
+            factor, delta = terms[j]
+            q0, g0 = apart(qg_all[h, 2 * half + j].reshape(ROWS, TOK))
             cols = slice(j * ROWS, (j + 1) * ROWS)
             dq = jnp.zeros((HEAD_DIM, ROWS), F32)
             for c in range(KEYS // CHUNK):
@@ -236,39 +251,89 @@
                 per = ROWS // CHUNK
                 at = c % per * CHUNK
                 dq += dot(kt_all[h, c // per, :, at : at + CHUNK], ds, NN)
-            dq = (dq * SCALE).astype(BF)
-            for i in range(2):
-                dq_st[h, 2 * half + j, i] = dq[:, i * ROWS // 2 : (i + 1) * ROWS // 2]
+            keep_dq(h, 2 * half + j, dq)
         if half == 1:
-            lane = lax.broadcasted_iota(jnp.int32, (ROWS, TOK), 1)
             for k in range(SIDE):
-                rows = slice(k * ROWS, (k + 1) * ROWS)
-                dkv = (acc[rows, :] * jnp.where(lane < HEAD_DIM, SCALE, 1.0)).astype(BF)
-                dkv_st[h, k] = dkv.reshape(2, ROWS // 2, TOK)
-            for copy in copies_r1(h):
+                keep_dkv(h, k, acc[k * ROWS : (k + 1) * ROWS, :])
+            for copy in copies_r1(h, 0) + copies_r1(h, 1):
                 copy.start()
 
-    def combine(h):
+    def combine_q(h):
         arrived(r1_q.at[h], r_r.at[0, h])
+        for n, t in enumerate((fwd(y, 1), back(y, 1))):
+            dq_st[h, t, n] = (dq_st[h, t, n].astype(F32) + r1_q[h, n].astype(F32)).astype(BF)
+        for copy in copies_r2(h, 0):
+            copy.start()
+
+    def combine_kv(h):
         arrived(r1_kv.at[h], r_r.at[1, h])
-        for n, (ty, tz) in enumerate(((fwd(y, 1), fwd(z, 1)), (back(y, 1), back(z, 1)))):
-            dq_st[h, ty, n] = (dq_st[h, ty, n].astype(F32) + r1_q[h, n].astype(F32)).astype(BF)
-            dkv_st[h, tz, n] = (dkv_st[h, tz, n].astype(F32) + r1_kv[h, n].astype(F32)).astype(BF)
-        for copy in copies_r2(h):
+        for n, t in enumerate((fwd(z, 1), back(z, 1))):
+            dkv_st[h, t, n] = (dkv_st[h, t, n].astype(F32) + r1_kv[h, n].astype(F32)).astype(BF)
+        for copy in copies_r2(h, 1):
             copy.start()
+
+    def last_unit():
+        h = HG - 1
+        terms = row_terms(2 * h + 1)
+        q0, g0 = apart(qg_all[h, 2:4].reshape(2 * ROWS, TOK))
+
+        def scores(k, dqs):
+            out = []
+            for j, dq in enumerate(dqs):
+                factor, delta = terms[j]
+                cols = slice(j * ROWS, (j + 1) * ROWS)
+                for c in range(ROWS // CHUNK):
+                    rows = pl.ds(pl.multiple_of(k * ROWS + c * CHUNK, CHUNK), CHUNK)
+                    p = p_ref[1, rows, cols].astype(F32) * factor
+                    ds = (p * (dp_ref[1, rows, cols] - delta)).astype(BF)
+                    p_ref[1, rows, cols] = p.astype(BF)
+                    p_ref[0, rows, cols] = ds
+                    dq += dot(kt_all[h, k, :, c * CHUNK : (c + 1) * CHUNK], ds, NN)
+                out.append(dq)
+            return out
+
+        def sums(k):
+            rows = pl.ds(pl.multiple_of(k * ROWS, ROWS), ROWS)
+            keep_dkv(h, k, acc[rows, :] + dot(p_ref[1, rows, :], g0, NN) + dot(p_ref[0, rows, :], q0, NN))
+
+        dqs = [jnp.zeros((HEAD_DIM, ROWS), F32)] * 2
+        far, near, own = fwd(z, 2), (fwd(z, 1), back(z, 1)), z
+        dqs = scores(far, dqs)
+        sums(far)
+        for copy in copies_r1(h, 1):
+            copy.start()
+        for k in near + (own,):
+            dqs = scores(k, dqs)
+        for j in range(2):
+            keep_dq(h, 2 + j, dqs[j])
+        for copy in copies_r1(h, 0):
+            copy.start()
+        for k in near:
+            sums(k)
+        hand_over(HG - 2)
+        combine_kv(h)
+        combine_q(h)
+        sums(own)
 
     def hand_over(h):
         arrived(r2_q.at[h], r_r.at[2, h])
-        arrived(r2_kv.at[h], r_r.at[3, h])
         for i in range(2):
             dq = dq_st[h, y, i].astype(F32) + r2_q[h, 0, i].astype(F32) + r2_q[h, 1, i].astype(F32)
+            for k in range(2):
+                g_q[h, 2 * i + k] = dq[:, k * TOK : (k + 1) * TOK].astype(BF)
+        for r in (2, 1, 3):
+            copy_g(h, r, 0).start()
+        for i in range(2):
+            arrived(r2_kv.at[h, 0], r_r.at[3 + i, h])
             dkv = dkv_st[h, z, i].astype(F32) + r2_kv[h, 0, i].astype(F32) + r2_kv[h, 1, i].astype(F32)
             for k in range(2):
-                g_q[h, 2 * i + k] = dq[:, k * TOK : (k + 1) * TOK].astype(BF)
                 g_kv[h, 2 * i + k] = dkv[k * TOK : (k + 1) * TOK, :].astype(BF)
-        for r in others:
-            for copy in copies_g(h, r):
-                copy.start()
+            for r in (2, 1, 3):
+
+                @pl.when(fwd(x, r) // 2 == i)
+                def _():
+                    copy_g(h, r, 1).start()
+
         f_q[HG * x + h] = g_q[h, x]
         f_kv[HG * x + h] = g_kv[h, x]
 
@@ -278,23 +343,19 @@
     forward(0)
 
     def step(h, carry):
-        @pl.when(h < HG)
-        def _():
-            receive(h)
+        receive(h)
 
         @pl.when(h < HG - 2)
         def _():
             start_a(h + 2)
 
-        @pl.when(h < HG)
-        def _():
-            phase1(h, 0)
+        phase1(h, 0)
 
         @pl.when(h < HG - 1)
         def _():
             spread(h + 1)
 
-        @pl.when((h > 1) & (h < HG))
+        @pl.when(h > 1)
         def _():
             hand_over(h - 2)
 
@@ -302,33 +363,23 @@
         def _():
             phase2(h - 1, 1)
 
-        @pl.when(h < HG)
-        def _():
-            phase1(h, 1)
+        phase1(h, 1)
 
         @pl.when(h < HG - 1)
         def _():
             forward(h + 1)
 
-        @pl.when(h == HG)
-        def _():
-            hand_over(HG - 2)
-
         @pl.when(h > 0)
         def _():
-            combine(h - 1)
-
-        @pl.when(h < HG)
-        def _():
-            phase2(h, 0)
-
-        @pl.when(h == HG)
-        def _():
-            hand_over(HG - 1)
-
+            combine_q(h - 1)
+            combine_kv(h - 1)
+
+        phase2(h, 0)
         return carry
 
-    lax.fori_loop(0, HG + 1, step, 0)
+    lax.fori_loop(0, HG, step, 0)
+    last_unit()
+    hand_over(HG - 1)
 
     def finish(h, carry):
         arrived(g_q.at[h, pl.ds(0, SIDE - 1)], g_r.at[0, h])
@@ -400,7 +451,7 @@
         ]
         + [
             pltpu.SemaphoreType.DMA(shape)
-            for shape in [(10,), (HG, SIDE - 1), (HG, SIDE), (HG,), (2 * HG,), (4, HG), (2, HG)]
+            for shape in [(10,), (HG, SIDE - 1), (HG, SIDE), (HG,), (2 * HG,), (5, HG), (2, HG)]
         ],
         compiler_params=pltpu.CompilerParams(
             collective_id=0, has_side_effects=True, vmem_limit_bytes=60 * 2**20

time: 111 us -> 110 us (level)
  no operation moved by 1% of the time
where the time goes in v5:
time: 110 us
  Pallas kernels  106 us (96%)
  local copies, waits for them, and re-layouts  2.81 us (3%)
  between operations  1.3 us (1%)
    pallas_call x1, Pallas kernels, body(): pl.pallas_call(kernel, out_shape=(jax.ShapeDtypeStruct(image_qkv.shape, B...  106 us
    unnamed x4, local copies, waits for them, and re-layouts  2.81 us

profile of v5, /device:TPU:0, one launch (start us, length us, event | category | flops | bytes accessed | tf_op | source)
XLA Modules:
  0.0 109.9 jit_solution(3635904445734110298)
XLA Ops:
  1.3 105.8 %shard_map.68 = (bf16[3,120,1216]{2,1,0:T(8,128)(2,1)}, bf16[3,8,1216]{2,1,0:T(8,128)(2,1)}) custom-call(s32[1]{0:T(128)S(6)} %copy.9.tl_ref, bf16[3,120,1216]{2,1,0:T(8,128)(2,1)} %image_qkv.1, bf16[3,8,1216]{2,1,0:T(8,128)(2,1)} %text_qkv.1, bf16[120,1216]{1,0:T(8,128)(2,1)} %image_grad.1, bf16[8,1216]{1,0:T(8,128)(2,1)} %text_grad.1), custom_call_target="tpu_custom_call" | custom-call | tf_op jit(solution)/shard_map/pallas_call | solution.py:422
  107.1 0.0 copy-start
  107.1 2.2 %copy.10 = bf16[3,120,1216]{2,1,0:T(8,128)(2,1)} copy(bf16[3,120,1216]{2,1,0:T(8,128)(2,1)} %get-tuple-element.4) | data formatting | bytes 1751040
  109.3 0.0 copy-done
  109.3 0.6 copy.11
Async XLA Ops:
  107.1 2.2 %copy-start = (bf16[3,8,1216]{2,1,0:T(8,128)(2,1)S(1)}, bf16[3,8,1216]{2,1,0:T(8,128)(2,1)}, u32[]{:S(2)}) copy-start(bf16[3,8,1216]{2,1,0:T(8,128)(2,1)} %get-tuple-element.5) | copy-start | bytes 175108

commit v6 on v5

--- a/solution.py
+++ b/solution.py
@@ -349,11 +349,15 @@
         def _():
             start_a(h + 2)
 
+        @pl.when((h > 0) & (h < HG - 1))
+        def _():
+            spread(h + 1)
+
         phase1(h, 0)
 
-        @pl.when(h < HG - 1)
-        def _():
-            spread(h + 1)
+        @pl.when(h == 0)
+        def _():
+            spread(1)
 
         @pl.when(h > 1)
         def _():
@@ -363,11 +367,15 @@
         def _():
             phase2(h - 1, 1)
 
+        @pl.when((h > 0) & (h < HG - 1))
+        def _():
+            forward(h + 1)
+
         phase1(h, 1)
 
-        @pl.when(h < HG - 1)
-        def _():
-            forward(h + 1)
+        @pl.when(h == 0)
+        def _():
+            forward(1)
 
         @pl.when(h > 0)
         def _():

time: 110 us -> 108 us (0.982)
  Pallas kernels: 106 us -> 104 us
    pallas_call x1, Pallas kernels: 106 us -> 104 us  [body(): pl.pallas_call(kernel, out_shape=(jax.ShapeDtypeStruct(image_qkv.shape, B...]
where the time goes in v6:
time: 108 us
  Pallas kernels  104 us (96%)
  local copies, waits for them, and re-layouts  2.81 us (3%)
  between operations  1.3 us (1%)
    pallas_call x1, Pallas kernels, body(): pl.pallas_call(kernel, out_shape=(jax.ShapeDtypeStruct(image_qkv.shape, B...  104 us
    unnamed x4, local copies, waits for them, and re-layouts  2.81 us

profile of v6, /device:TPU:0, one launch (start us, length us, event | category | flops | bytes accessed | tf_op | source)
XLA Modules:
  0.0 108.3 jit_solution(11906286561772118114)
XLA Ops:
  1.3 104.2 %shard_map.68 = (bf16[3,120,1216]{2,1,0:T(8,128)(2,1)}, bf16[3,8,1216]{2,1,0:T(8,128)(2,1)}) custom-call(s32[1]{0:T(128)S(6)} %copy.9.tl_ref, bf16[3,120,1216]{2,1,0:T(8,128)(2,1)} %image_qkv.1, bf16[3,8,1216]{2,1,0:T(8,128)(2,1)} %text_qkv.1, bf16[120,1216]{1,0:T(8,128)(2,1)} %image_grad.1, bf16[8,1216]{1,0:T(8,128)(2,1)} %text_grad.1), custom_call_target="tpu_custom_call" | custom-call | tf_op jit(solution)/shard_map/pallas_call | solution.py:430
  105.5 0.0 copy-start
  105.5 2.2 %copy.10 = bf16[3,120,1216]{2,1,0:T(8,128)(2,1)} copy(bf16[3,120,1216]{2,1,0:T(8,128)(2,1)} %get-tuple-element.4) | data formatting | bytes 1751040
  107.7 0.0 copy-done
  107.7 0.6 copy.11
Async XLA Ops:
  105.5 2.2 %copy-start = (bf16[3,8,1216]{2,1,0:T(8,128)(2,1)S(1)}, bf16[3,8,1216]{2,1,0:T(8,128)(2,1)}, u32[]{:S(2)}) copy-start(bf16[3,8,1216]{2,1,0:T(8,128)(2,1)} %get-tuple-element.5) | copy-start | bytes 175108

commit v7 on v6

--- a/solution.py
+++ b/solution.py
@@ -385,16 +385,34 @@
         phase2(h, 0)
         return carry
 
-    lax.fori_loop(0, HG, step, 0)
-    last_unit()
-    hand_over(HG - 1)
+    image_rows = image_grad.shape[0]
+
+    def assemble(some):
+        for pair in some:
+            both = 2 * pair + 1 < heads
+            width = TOK if both else HEAD_DIM
+            cols = slice(pair * TOK, pair * TOK + width)
+            first, second = f_kv[2 * pair].astype(F32), f_kv[2 * pair + 1].astype(F32)
+            query = jnp.concatenate([f_q[2 * pair], f_q[2 * pair + 1]], 0).astype(F32).T
+            key = jnp.concatenate([first[:, :HEAD_DIM], second[:, :HEAD_DIM]], 1)
+            value = jnp.concatenate([first[:, HEAD_DIM:], second[:, HEAD_DIM:]], 1)
+            for i, whole in enumerate((query, key, value)):
+                image_out[i, :, cols] = whole[:image_rows, :width].astype(BF)
+                text_out[i, :, cols] = whole[image_rows:, :width].astype(BF)
 
     def finish(h, carry):
         arrived(g_q.at[h, pl.ds(0, SIDE - 1)], g_r.at[0, h])
         arrived(g_kv.at[h, pl.ds(0, SIDE - 1)], g_r.at[1, h])
         return carry
 
-    lax.fori_loop(0, HG, finish, 0)
+    pairs = range((heads + 1) // 2)
+    late = {(HG * g + HG - 1) // 2 for g in range(SIDE)}
+    lax.fori_loop(0, HG, step, 0)
+    last_unit()
+    lax.fori_loop(0, HG - 1, finish, 0)
+    assemble(pair for pair in pairs if pair not in late)
+    hand_over(HG - 1)
+    finish(HG - 1, 0)
     moved = (
         qg_all.at[:, pl.ds(0, 2), pl.ds(0, SIDE - 1)],
         qg_all,
@@ -410,18 +428,7 @@
     for i, ref in enumerate(moved):
         gone(ref, sent.at[i])
 
-    image_rows = image_grad.shape[0]
-    for pair in range((heads + 1) // 2):
-        both = 2 * pair + 1 < heads
-        width = TOK if both else HEAD_DIM
-        cols = slice(pair * TOK, pair * TOK + width)
-        first, second = f_kv[2 * pair].astype(F32), f_kv[2 * pair + 1].astype(F32)
-        query = jnp.concatenate([f_q[2 * pair], f_q[2 * pair + 1]], 0).astype(F32).T
-        key = jnp.concatenate([first[:, :HEAD_DIM], second[:, :HEAD_DIM]], 1)
-        value = jnp.concatenate([first[:, HEAD_DIM:], second[:, HEAD_DIM:]], 1)
-        for i, whole in enumerate((query, key, value)):
-            image_out[i, :, cols] = whole[:image_rows, :width].astype(BF)
-            text_out[i, :, cols] = whole[image_rows:, :width].astype(BF)
+    assemble(pair for pair in pairs if pair in late)
 
 
 def body(image_qkv, text_qkv, image_grad, text_grad, text_len):

time: 108 us -> 108 us (level)
  no operation moved by 1% of the time
where the time goes in v7:
time: 108 us
  Pallas kernels  104 us (96%)
  local copies, waits for them, and re-layouts  2.81 us (3%)
  between operations  1.3 us (1%)
    pallas_call x1, Pallas kernels, body(): pl.pallas_call(kernel, out_shape=(jax.ShapeDtypeStruct(image_qkv.shape, B...  104 us
    unnamed x4, local copies, waits for them, and re-layouts  2.81 us

profile of v7, /device:TPU:0, one launch (start us, length us, event | category | flops | bytes accessed | tf_op | source)
XLA Modules:
  0.0 108.2 jit_solution(12457325092814134887)
XLA Ops:
  1.3 104.1 %shard_map.68 = (bf16[3,120,1216]{2,1,0:T(8,128)(2,1)}, bf16[3,8,1216]{2,1,0:T(8,128)(2,1)}) custom-call(s32[1]{0:T(128)S(6)} %copy.9.tl_ref, bf16[3,120,1216]{2,1,0:T(8,128)(2,1)} %image_qkv.1, bf16[3,8,1216]{2,1,0:T(8,128)(2,1)} %text_qkv.1, bf16[120,1216]{1,0:T(8,128)(2,1)} %image_grad.1, bf16[8,1216]{1,0:T(8,128)(2,1)} %text_grad.1), custom_call_target="tpu_custom_call" | custom-call | tf_op jit(solution)/shard_map/pallas_call | solution.py:437
  105.4 0.0 copy-start
  105.4 2.2 %copy.10 = bf16[3,120,1216]{2,1,0:T(8,128)(2,1)} copy(bf16[3,120,1216]{2,1,0:T(8,128)(2,1)} %get-tuple-element.4) | data formatting | bytes 1751040
  107.6 0.0 copy-done
  107.6 0.6 copy.11
Async XLA Ops:
  105.4 2.2 %copy-start = (bf16[3,8,1216]{2,1,0:T(8,128)(2,1)S(1)}, bf16[3,8,1216]{2,1,0:T(8,128)(2,1)}, u32[]{:S(2)}) copy-start(bf16[3,8,1216]{2,1,0:T(8,128)(2,1)} %get-tuple-element.5) | copy-start | bytes 175108
